TPU v7x, 128 devices: a whole 4x4x4 slice. The times are simulated.
128 devices in a mesh: blk: 64 (over z, y, x), grid: 2 (over core).
Axes of the slice: x: 4, y: 4, z: 4, core: 2. Of those that a mesh axis runs over, the one named last changes fastest.
Arguments:
- orbitals: bfloat16 [2048, 64, 4096], P('blk', 'grid'), may hold values from -6 to 6
- pair_first: int32 [64, 4], P('blk'), may hold values from 0 to 31
- pair_second: int32 [64, 4], P('blk'), may hold values from 0 to 31
- pair_count: int32 [64], P('blk'), may hold values from 1 to 4, as said below
Outputs:
- exchange: bfloat16 [2048, 64, 4096], P('blk', 'grid')
Inputs may be any that keep to these rules, and one draw needn't show every extreme that they name: `pair_count`: some block has exactly 4 live slots in every draw.
All inputs are finite; a program needn't handle non-finite values.
Results may differ from a plain program's by a relative error of at most 0.002.
Values may be sent and summed in bfloat16 or wider, within the bound.
A program may use at most 192 MiB of HBM per device.

v0:
```python
import math

import jax
import jax.numpy as jnp
from jax import lax
from jax.sharding import PartitionSpec as P

spacing = 0.5
fraction = 0.25
highest = lax.Precision.HIGHEST


def from_behind(value, axis, steps):
    count = lax.axis_size(axis)
    pairs = [(source, (source + steps) % count) for source in range(count)]
    return lax.ppermute(value, axis, pairs)


def dft_tables(length):
    positions = jnp.arange(length, dtype=jnp.int32)
    phases = positions[:, None] * positions[None, :] % length
    angles = phases.astype(jnp.float32) * (2.0 * math.pi / length)
    cosine = jnp.cos(angles)
    sine_table = jnp.sin(angles)
    forward = jnp.concatenate(
        [jnp.concatenate([cosine, -sine_table], 1), jnp.concatenate([sine_table, cosine], 1)], 0
    )
    inverse = jnp.concatenate(
        [jnp.concatenate([cosine, sine_table], 1), jnp.concatenate([-sine_table, cosine], 1)], 0
    )
    return ((cosine, sine_table), forward, inverse)


def rotate_parts(values):
    half_width = values.shape[-1] // 2
    return jnp.concatenate([values[..., half_width:], -values[..., :half_width]], -1)


def transform_axis(tables, values, pattern, sign_factor):
    direct = jnp.einsum(pattern, tables[0], values, precision=highest)
    turned = jnp.einsum(pattern, tables[1], rotate_parts(values), precision=highest)
    return direct + sign_factor * turned


def pencil_kernel(length, grid_index, groups):
    pencil_width = length // groups
    positions = jnp.arange(length, dtype=jnp.int32)
    wrapped = jnp.where(positions >= length // 2, positions - length, positions).astype(jnp.float32)
    squares = (wrapped * (2.0 * math.pi / (length * spacing))) ** 2
    local_squares = lax.dynamic_slice_in_dim(squares, grid_index * pencil_width, pencil_width)
    square_sum = squares[:, None, None] + local_squares[None, :, None] + squares[None, None, :]
    at_anchor = square_sum <= 0.0
    kernel = jnp.where(
        at_anchor, 0.0, 4.0 * math.pi / jnp.where(at_anchor, 1.0, square_sum)
    ) / float(length**3)
    return jnp.concatenate([kernel, kernel], -1)


def pencil_solve(values, tables, kernel):
    values = transform_axis(tables, values, "kx,nxyw->nkyw", 1.0)
    return transform_axis(tables, values * kernel, "kx,nxyw->nkyw", -1.0)


def pair_group(own_rows, visit_rows, live_mask, tables, forward, inverse, transform):
    group_size, slab_rows, plane_cells = own_rows.shape
    length = forward.shape[0] // 2
    density = (own_rows * visit_rows).reshape(group_size, slab_rows, length, length)
    spectra = jnp.einsum("nxyz,zw->nxyw", density, forward[:length], precision=highest)
    spectra = transform_axis(tables, spectra, "ky,nxyw->nxkw", 1.0)
    spectra = transform(spectra)
    spectra = transform_axis(tables, spectra, "ky,nxyw->nxkw", -1.0)
    potential = jnp.einsum("nxyw,wz->nxyz", spectra, inverse[:, :length], precision=highest)
    potential = (
        potential.reshape(group_size, slab_rows * plane_cells) * (-fraction * live_mask)[:, None]
    )
    own_flat = own_rows.reshape(group_size, slab_rows * plane_cells)
    visit_flat = visit_rows.reshape(group_size, slab_rows * plane_cells)
    return (potential * visit_flat, potential * own_flat)


def per_device(orbitals, pair_first, pair_second, pair_count):
    block_size, slab_rows, plane_cells = orbitals.shape
    length = math.isqrt(plane_cells)
    first_index = pair_first[0]
    second_index = pair_second[0]
    live_count = pair_count[0]
    slot_total = first_index.shape[0]
    visiting = from_behind(orbitals, "blk", 1)
    tables, forward, inverse = dft_tables(length)
    kernel = pencil_kernel(length, lax.axis_index("grid"), lax.axis_size("grid"))
    group_size = 1
    flat_cells = slab_rows * plane_cells
    own_empty = jnp.zeros((block_size, flat_cells), jnp.float32)
    back_empty = jnp.zeros((block_size, flat_cells), jnp.float32)

    def select_rows(firsts, seconds):
        own_rows = jnp.take(orbitals, firsts, axis=0).astype(jnp.float32)
        visit_rows = jnp.take(visiting, seconds, axis=0).astype(jnp.float32)
        return (own_rows, visit_rows, seconds)

    def solve_slot(values):
        return lax.all_to_all(
            pencil_solve(values, tables, kernel), "grid", split_axis=1, concat_axis=2, tiled=True
        )

    def transform_slot(values):
        return solve_slot(lax.all_to_all(values, "grid", split_axis=2, concat_axis=1, tiled=True))

    turn_count = slot_total // group_size

    def slot_step(turn_index, totals):
        first_slot = turn_index * group_size
        firsts = lax.dynamic_slice_in_dim(first_index, first_slot, group_size)
        seconds = lax.dynamic_slice_in_dim(second_index, first_slot, group_size)
        slot_numbers = first_slot + jnp.arange(group_size, dtype=jnp.int32)
        live_mask = (slot_numbers < live_count).astype(jnp.float32)
        own_rows, visit_rows, target = select_rows(firsts, seconds)
        own_slot, back_slot = pair_group(
            own_rows, visit_rows, live_mask, tables, forward, inverse, transform_slot
        )
        return (totals[0].at[firsts].add(own_slot), totals[1].at[target].add(back_slot))

    own_total, back_store = lax.fori_loop(0, turn_count, slot_step, (own_empty, back_empty))
    back_rows = back_store.astype(jnp.bfloat16)
    returned = from_behind(back_rows, "blk", -1)
    merged = own_total + returned.astype(jnp.float32)
    return merged.reshape(orbitals.shape).astype(jnp.bfloat16)


def solution(mesh):
    return jax.shard_map(
        per_device,
        mesh=mesh,
        in_specs=(P("blk", "grid", None), P("blk", None), P("blk", None), P("blk")),
        out_specs=P("blk", "grid", None),
        check_vma=False,
    )
```

profile of v0, /device:TPU:0, one launch (start us, length us, event | category | flops | bytes accessed | tf_op | source)
XLA Modules:
  0.0 665.3 jit_solution(17335487089337337582)
XLA Ops:
  3.9 185.6 %collective-permute-done = bf16[32,32,4096]{2,1,0:T(8,128)(2,1)} collective-permute-done((bf16[32,32,4096]{2,1,0:T(8,128)(2,1)}, bf16[32,32,4096]{2,1,0:T(8,128)(2,1)}, u32[]{:S(2)}, u32[]{:S(2)}) %collective-permute-start) | collective-permute-done | bytes 8388640 | tf_op jit(solution)/shard_map/ppermute | solution.py:16
  189.5 6.8 %broadcast.166.clone = f32[32,131072]{1,0:T(8,128)} broadcast(f32[]{:T(128)} %constant.167.clone.1), dimensions={} | broadcast | bytes 16777220 | tf_op jit(solution)/shard_map/broadcast.7
  196.3 6.8 %broadcast.166 = f32[32,131072]{1,0:T(8,128)} broadcast(f32[]{:T(128)} %constant.167.clone.1), dimensions={} | broadcast | bytes 16777220 | tf_op jit(solution)/shard_map/broadcast.7
  203.2 257.3 %while.20 = (s32[]{:T(128)}, f32[32,131072]{1,0:T(8,128)}, f32[32,131072]{1,0:T(8,128)}, s32[4]{0:T(128)S(1)}, bf16[32,32,4096]{2,1,0:T(8,128)(2,1)}, /*index=5*...) while((s32[]{:T(128)}, f32[32,131072]{1,0:T(8,128)}, ...), condition=%wide.region_3.5_spmd.clone.clone, body=%wide.region_0.4_spmd.clone.clone.sunk | while | flops 2019229696 | bytes 59834792 | solution.py:123
  214.4 4.6 all_to_all.80
  239.9 6.1 broadcast_select_fusion.3
  246.0 10.8 %scatter-add.16 = f32[32,131072]{1,0:T(8,128)} dynamic-update-slice(f32[32,131072]{1,0:T(8,128)} %get-tuple-element.533, f32[1,131072]{1,0:T(1,128)S(1)} %get-tuple-element.511, s32[]{:T(128)} %bitcast.164, s32[]{:T(128)} %constant.166.clone.1..sunk) | dynamic-update-slice | bytes 1048580 | tf_op jit(solution)/shard_map/while/body/eval_jaxpr/scatter-add | solution.py:121
  256.8 10.8 %scatter-add.17 = f32[32,131072]{1,0:T(8,128)} dynamic-update-slice(f32[32,131072]{1,0:T(8,128)} %get-tuple-element.534, f32[1,131072]{1,0:T(1,128)S(1)} %get-tuple-element.512, s32[]{:T(128)} %bitcast.166, s32[]{:T(128)} %constant.166.clone.1..sunk) | dynamic-update-slice | bytes 1048580 | tf_op jit(solution)/shard_map/while/body/eval_jaxpr/scatter-add | solution.py:121
  278.6 4.6 all_to_all.80
  304.1 6.1 broadcast_select_fusion.3
  310.2 10.9 %scatter-add.16 = f32[32,131072]{1,0:T(8,128)} dynamic-update-slice(f32[32,131072]{1,0:T(8,128)} %get-tuple-element.533, f32[1,131072]{1,0:T(1,128)S(1)} %get-tuple-element.511, s32[]{:T(128)} %bitcast.164, s32[]{:T(128)} %constant.166.clone.1..sunk) | dynamic-update-slice | bytes 1048580 | tf_op jit(solution)/shard_map/while/body/eval_jaxpr/scatter-add | solution.py:121
  321.1 10.8 %scatter-add.17 = f32[32,131072]{1,0:T(8,128)} dynamic-update-slice(f32[32,131072]{1,0:T(8,128)} %get-tuple-element.534, f32[1,131072]{1,0:T(1,128)S(1)} %get-tuple-element.512, s32[]{:T(128)} %bitcast.166, s32[]{:T(128)} %constant.166.clone.1..sunk) | dynamic-update-slice | bytes 1048580 | tf_op jit(solution)/shard_map/while/body/eval_jaxpr/scatter-add | solution.py:121
  342.9 4.6 all_to_all.80
  368.4 6.1 broadcast_select_fusion.3
  374.5 10.8 %scatter-add.16 = f32[32,131072]{1,0:T(8,128)} dynamic-update-slice(f32[32,131072]{1,0:T(8,128)} %get-tuple-element.533, f32[1,131072]{1,0:T(1,128)S(1)} %get-tuple-element.511, s32[]{:T(128)} %bitcast.164, s32[]{:T(128)} %constant.166.clone.1..sunk) | dynamic-update-slice | bytes 1048580 | tf_op jit(solution)/shard_map/while/body/eval_jaxpr/scatter-add | solution.py:121
  385.4 10.9 %scatter-add.17 = f32[32,131072]{1,0:T(8,128)} dynamic-update-slice(f32[32,131072]{1,0:T(8,128)} %get-tuple-element.534, f32[1,131072]{1,0:T(1,128)S(1)} %get-tuple-element.512, s32[]{:T(128)} %bitcast.166, s32[]{:T(128)} %constant.166.clone.1..sunk) | dynamic-update-slice | bytes 1048580 | tf_op jit(solution)/shard_map/while/body/eval_jaxpr/scatter-add | solution.py:121
  407.2 4.6 all_to_all.80
  432.7 6.1 broadcast_select_fusion.3
  438.8 10.8 %scatter-add.16 = f32[32,131072]{1,0:T(8,128)} dynamic-update-slice(f32[32,131072]{1,0:T(8,128)} %get-tuple-element.533, f32[1,131072]{1,0:T(1,128)S(1)} %get-tuple-element.511, s32[]{:T(128)} %bitcast.164, s32[]{:T(128)} %constant.166.clone.1..sunk) | dynamic-update-slice | bytes 1048580 | tf_op jit(solution)/shard_map/while/body/eval_jaxpr/scatter-add | solution.py:121
  449.7 10.8 %scatter-add.17 = f32[32,131072]{1,0:T(8,128)} dynamic-update-slice(f32[32,131072]{1,0:T(8,128)} %get-tuple-element.534, f32[1,131072]{1,0:T(1,128)S(1)} %get-tuple-element.512, s32[]{:T(128)} %bitcast.166, s32[]{:T(128)} %constant.166.clone.1..sunk) | dynamic-update-slice | bytes 1048580 | tf_op jit(solution)/shard_map/while/body/eval_jaxpr/scatter-add | solution.py:121
  460.5 6.5 convert_element_type.75
  468.7 181.1 %collective-permute-done.1 = bf16[32,131072]{1,0:T(8,128)(2,1)S(1)} collective-permute-done((bf16[32,131072]{1,0:T(8,128)(2,1)S(1)}, bf16[32,131072]{1,0:T(8,128)(2,1)S(1)}, u32[]{:S(2)}, u32[]{:S(2)}) %collective-permute-start.1) | collective-permute-done | bytes 8388640 | tf_op jit(solution)/shard_map/ppermute | solution.py:16
  649.9 4.0 add_convert_fusion
  653.8 11.5 %copy.17 = bf16[4,8,32,4096]{3,2,1,0:T(8,128)(2,1)} copy(bf16[4,8,32,4096]{3,1,2,0:T(8,128)(2,1)} %bitcast.188) | data formatting | bytes 16777216
  (136 shorter events, 115.3 us)
Async XLA Ops:
  0.0 189.5 %collective-permute-start = (bf16[32,32,4096]{2,1,0:T(8,128)(2,1)}, bf16[32,32,4096]{2,1,0:T(8,128)(2,1)}, u32[]{:S(2)}, u32[]{:S(2)}) collective-permute-start(bf16[32,32,4096]{2,1,0:T(8,128)(2,1)} %param.12), channel_id=1, source_target_pairs={{0,2},{2,4},{4,6},{6,8},{8,10},{10,12},{12,14},{14,16},{16,18},{18... | collective-permute-start | bytes 25165832 | tf_op jit(solution)/shard_map/ppermute | solution.py:16
  189.5 13.6 %copy-start.1 = (s32[2]{0:T(128)S(1)}, s32[2]{0:T(128)}, u32[]{:S(2)}) copy-start(s32[2]{0:T(128)} %constant.160.clone.3) | copy-start | bytes 28
  189.5 13.6 %copy-start.2 = (s32[1,4]{1,0:T(1,128)S(1)}, s32[1,4]{1,0:T(1,128)}, u32[]{:S(2)}) copy-start(s32[1,4]{1,0:T(1,128)} %param.13) | copy-start | bytes 52
  189.5 13.6 %copy-start.3 = (s32[1,4]{1,0:T(1,128)S(1)}, s32[1,4]{1,0:T(1,128)}, u32[]{:S(2)}) copy-start(s32[1,4]{1,0:T(1,128)} %param.14) | copy-start | bytes 52
  227.9 6.6 all-to-all-start.1
  292.2 6.6 all-to-all-start.1
  356.5 6.6 all-to-all-start.1
  420.8 6.6 all-to-all-start.1
  460.5 189.4 %copy-start = (f32[32,131072]{1,0:T(8,128)S(1)}, f32[32,131072]{1,0:T(8,128)}, u32[]{:S(2)}) copy-start(f32[32,131072]{1,0:T(8,128)} %get-tuple-element.283) | copy-start | bytes 50331652
  466.9 182.9 %collective-permute-start.1 = (bf16[32,131072]{1,0:T(8,128)(2,1)S(1)}, bf16[32,131072]{1,0:T(8,128)(2,1)S(1)}, u32[]{:S(2)}, u32[]{:S(2)}) collective-permute-start(bf16[32,131072]{1,0:T(8,128)(2,1)S(1)} %convert_element_type.75), channel_id=1, source_target_pairs={{0,126},{2,0},{4,2},{6,4},{8,6},{10,8},{12,10},{14,12},{16,14},{18... | collective-permute-start | bytes 25165832 | tf_op jit(solution)/shard_map/ppermute | solution.py:16
where the time goes:
time: 669 us; the launch traced here: 665 us
  waiting for transfers between devices  367 us (55%)
  local copies, waits for them, and re-layouts  135 us (20%)
  other arithmetic  55.5 us (8%)
  matrix products  53.8 us (8%)
  loops' own time  18.4 us (3%)
  blocking collectives  18.3 us (3%)
  starting transfers between devices  17.7 us (3%)
    ppermute x2, waiting for transfers between devices, from_behind(): return lax.ppermute(value, axis, pairs)  367 us
    scatter-add x4, local copies, waits for them, and re-layouts, slot_step(): totals[0].at[firsts].add(own_slot)  43.4 us
    scatter-add x4, local copies, waits for them, and re-layouts, slot_step(): totals[1].at[target].add(back_slot)  43.3 us
    dot_general x16, matrix products, transform_axis(): jnp.einsum(pattern, tables[1], rotate_parts(values), precision=highest)  27.5 us
    another operation x8, other arithmetic  27.4 us
    dot_general x16, matrix products, transform_axis(): direct = jnp.einsum(pattern, tables[0], values, precision=highest)  18.5 us
    another operation x1, loops' own time, per_device(): lax.fori_loop(0, turn_count, slot_step, (own_empty, back_empty))  18.4 us
    all_to_all x4, blocking collectives, transform_slot(): lax.all_to_all(values, 'grid', split_axis=2, concat_axis=1, tiled=True)  18.3 us
  transfers between devices with their start and end apart: 6, of which 2 were waited for; matrix products, arithmetic and copies ran while one was open for 2% of the time, Pallas kernels for 0%

commit v1 on v0

v1 whole, which is shorter than its diff:
```python
import functools
import math

import jax
import jax.numpy as jnp
import ml_dtypes
import numpy as np
from jax import lax
from jax.experimental import pallas as pl
from jax.experimental.pallas import tpu as pltpu
from jax.sharding import PartitionSpec as P

spacing = 0.5
fraction = 0.25
L = 64
HALF = L // 2
LANES = 128
ROWS = 17
MINE = 9
f32 = jnp.float32
bf16 = jnp.bfloat16


def split_table(table):
    high = table.astype(ml_dtypes.bfloat16)
    low = (table - high.astype(np.float64)).astype(ml_dtypes.bfloat16)
    return high, low


def lane_tables():
    position = np.arange(L)
    angle = 2.0 * np.pi * (np.outer(position, position) % L) / L
    sign = np.array([[1.0, 1.0], [1.0, -1.0]])
    real = np.kron(sign, np.cos(angle))
    imag = np.kron(sign, -np.sin(angle))
    forward = np.block([[real, imag], [-imag, real]])
    inverse = np.block([[real, -imag], [imag, real]])
    return np.stack(split_table(forward)), np.stack(split_table(inverse))


def row_tables():
    position = np.arange(L)
    angle = 2.0 * np.pi * (np.outer(position, position) % L) / L
    both = np.concatenate([np.cos(angle), np.sin(angle)], 0)
    forwards, inverses = [], []
    for core in range(2):
        order = np.concatenate([np.arange(HALF) + HALF * core, np.arange(HALF) + HALF * (1 - core)])
        high, low = split_table(both[:, order])
        forwards.append(np.concatenate([high, high, low], 1))
        back = np.concatenate([both[:L, order].T, both[L:, order].T], 0)
        high, low = split_table(back)
        inverses.append(np.concatenate([high, high, low], 1))
    return np.stack(forwards), np.stack(inverses)


def filter_table():
    wrapped = np.arange(L)
    wrapped = np.where(wrapped >= HALF, wrapped - L, wrapped)
    squares = (wrapped * (2.0 * np.pi / (L * spacing))) ** 2
    ky = np.arange(ROWS)[:, None] + HALF * np.arange(2)[None, :]
    total = squares[None, :, None, None] + squares[ky][:, None, :, None] + squares[None, None, None, :]
    kernel = np.where(total > 0, 4.0 * np.pi / np.where(total > 0, total, 1.0), 0.0)
    return (-fraction / L**3 * kernel).reshape(ROWS, L, LANES).astype(np.float32)


def twiddle_table():
    odd = np.repeat(np.arange(2), L)
    angle = 2.0 * np.pi * np.outer(np.arange(ROWS), odd) / L
    return np.stack([np.cos(angle), -np.sin(angle)], 1).astype(np.float32)


def real_forward(values):
    count = len(values)
    if count == 2:
        return [values[0] + values[1], values[0] - values[1]], [None, None]
    even_re, even_im = real_forward(values[0::2])
    odd_re, odd_im = real_forward(values[1::2])
    half, quarter = count // 2, count // 4
    re, im = [None] * (half + 1), [None] * (half + 1)
    re[0], re[half] = even_re[0] + odd_re[0], even_re[0] - odd_re[0]
    re[quarter], im[quarter] = even_re[quarter], -odd_re[quarter]
    for k in range(1, quarter):
        c, s = math.cos(2.0 * math.pi * k / count), math.sin(2.0 * math.pi * k / count)
        if 2 * k == quarter:
            turned_re, turned_im = c * (odd_re[k] + odd_im[k]), c * (odd_im[k] - odd_re[k])
        else:
            turned_re = c * odd_re[k] + s * odd_im[k]
            turned_im = c * odd_im[k] - s * odd_re[k]
        re[k], im[k] = even_re[k] + turned_re, even_im[k] + turned_im
        re[half - k], im[half - k] = even_re[k] - turned_re, turned_im - even_im[k]
    return re, im


def real_inverse(re, im):
    half = len(re) - 1
    count = 2 * half
    if count == 2:
        return [re[0] + re[1], re[0] - re[1]]
    quarter = half // 2
    even_re, even_im = [None] * (quarter + 1), [None] * (quarter + 1)
    odd_re, odd_im = [None] * (quarter + 1), [None] * (quarter + 1)
    even_re[0], odd_re[0] = re[0] + re[half], re[0] - re[half]
    even_re[quarter], odd_re[quarter] = 2.0 * re[quarter], -2.0 * im[quarter]
    for k in range(1, quarter):
        c, s = math.cos(2.0 * math.pi * k / count), math.sin(2.0 * math.pi * k / count)
        even_re[k], even_im[k] = re[k] + re[half - k], im[k] - im[half - k]
        part_re, part_im = re[k] - re[half - k], im[k] + im[half - k]
        if 2 * k == quarter:
            odd_re[k], odd_im[k] = c * (part_re - part_im), c * (part_re + part_im)
        else:
            odd_re[k] = c * part_re - s * part_im
            odd_im[k] = s * part_re + c * part_im
    evens, odds = real_inverse(even_re, even_im), real_inverse(odd_re, odd_im)
    return [value for pair in zip(evens, odds) for value in pair]


def split(values):
    high = values.astype(bf16)
    return high, (values - high.astype(f32)).astype(bf16)


def dot(left, right):
    return jnp.dot(left, right, preferred_element_type=f32)


def pair_kernel(
    blocks, slots,
    orbitals, second_in, count_in, first_s, second_s, count_s,
    lane_fwd, lane_inv, row_fwd, row_inv, filters, twiddles,
    own_out, back_out, next_second, next_count,
    orb, sending, visiting, own_terms, back_terms, back_rows,
    spectra_hi, spectra_lo, planes, others, filtered, returned, result,
    lane_fwd_v, lane_inv_v, row_fwd_v, row_inv_v, filters_v, twiddles_v,
    load_sem, table_sem, index_send, index_recv, visit_send, visit_recv,
    back_send, back_recv, own_sem, first_send, first_recv, second_send, second_recv,
):
    me, core = lax.axis_index("blk"), lax.axis_index("grid")
    right, left = lax.rem(me + 1, blocks), lax.rem(me + blocks - 1, blocks)
    to_right, to_left, to_partner = {"blk": right}, {"blk": left}, {"grid": 1 - core}

    load = pltpu.make_async_copy(orbitals, orb, load_sem)
    load.start()
    base = 8 * core
    tables = [
        pltpu.make_async_copy(source, target, table_sem.at[place])
        for place, (source, target) in enumerate([
            (lane_fwd, lane_fwd_v), (lane_inv, lane_inv_v),
            (row_fwd.at[core], row_fwd_v), (row_inv.at[core], row_inv_v),
            (filters.at[pl.ds(base, MINE)], filters_v), (twiddles, twiddles_v),
        ])
    ]
    for table in tables:
        table.start()

    barrier = pltpu.get_barrier_semaphore()
    for device in (to_right, to_left, to_partner):
        pl.semaphore_signal(barrier, inc=1, device_id=device)
    pl.semaphore_wait(barrier, 3)

    def remote(source, target, send, recv, device):
        return pltpu.make_async_remote_copy(
            src_ref=source, dst_ref=target, send_sem=send, recv_sem=recv, device_id=device
        )

    index_copies = [
        remote(second_in, next_second, index_send.at[0], index_recv.at[0], to_left),
        remote(count_in, next_count, index_send.at[1], index_recv.at[1], to_left),
    ]
    for copy in index_copies:
        copy.start()
    for copy in index_copies:
        copy.wait()
    load.wait()

    def visit_copy(slot):
        return remote(sending.at[slot], visiting.at[slot], visit_send.at[slot], visit_recv.at[slot], to_right)

    def back_copy(slot):
        return remote(back_rows.at[slot], back_out.at[slot], back_send.at[slot], back_recv.at[slot], to_left)

    def own_copy(slot):
        return pltpu.make_async_copy(own_terms.at[slot], own_out.at[slot], own_sem.at[slot])

    for slot in range(slots):
        sending[slot] = orb[next_second[0, slot]]
        visit_copy(slot).start()
    for table in tables:
        table.wait()

    other_base = 8 * (1 - core)
    first_copy = remote(planes.at[pl.ds(other_base, MINE)], others, first_send, first_recv, to_partner)
    second_copy = remote(
        filtered.at[pl.ds(core, 8)], returned.at[pl.ds(base + core, 8)], second_send, second_recv, to_partner
    )

    def one_slot(slot, carry):
        mine = first_s[0, slot]
        visit_copy(slot).wait_recv()

        def forward_group(group, carry):
            rows = pl.ds(pl.multiple_of(16 * group, 16), 16)
            values = []
            for column in range(HALF):
                lanes = pl.ds(LANES * column, LANES)
                values.append(orb[mine, rows, lanes].astype(f32) * visiting[slot, rows, lanes].astype(f32))
            re, im = real_forward(values)
            for k in range(ROWS):
                if k == 0:
                    turned_re, turned_im = re[0], jnp.zeros_like(re[0])
                else:
                    c, s = twiddles_v[k, 0:1], twiddles_v[k, 1:2]
                    if im[k] is None:
                        turned_re, turned_im = re[k] * c, re[k] * s
                    else:
                        turned_re, turned_im = re[k] * c - im[k] * s, re[k] * s + im[k] * c
                for part, value in enumerate((turned_re, turned_im)):
                    high, low = split(value)
                    spectra_hi[k, rows, LANES * part : LANES * (part + 1)] = high
                    spectra_lo[k, rows, LANES * part : LANES * (part + 1)] = low
            return carry

        lax.fori_loop(0, 2, forward_group, 0)

        def to_planes(start, count):
            where = pl.ds(start, count)
            high = spectra_hi[where].reshape(count * HALF, 2 * LANES)
            low = spectra_lo[where].reshape(count * HALF, 2 * LANES)
            out = dot(high, lane_fwd_v[0]) + dot(low, lane_fwd_v[0]) + dot(high, lane_fwd_v[1])
            planes[where] = out.reshape(count, HALF, 2 * LANES)

        to_planes(other_base, MINE)
        first_copy.start()
        to_planes(base + core, 8)
        first_copy.wait()

        def solve(k, carry):
            values = jnp.concatenate([planes[base + k], others[k]], 0)
            high, low = split(values)
            out = dot(row_fwd_v[...], jnp.concatenate([high, low, high], 0))
            kernel = filters_v[k]
            re = (out[:L, :LANES] + out[L:, LANES:]) * kernel
            im = (out[:L, LANES:] - out[L:, :LANES]) * kernel
            high, low = split(jnp.concatenate([re, im], 1))
            out = dot(row_inv_v[...], jnp.concatenate([high, low, high], 0))
            re = out[:L, :LANES] - out[L:, LANES:]
            im = out[:L, LANES:] + out[L:, :LANES]
            whole = jnp.concatenate([re, im], 1)
            returned[base + k] = whole[:HALF]
            filtered[k] = whole[HALF:]
            return carry

        lax.fori_loop(0, MINE, solve, 0)
        second_copy.start()

        def from_planes(start, count):
            where = pl.ds(start, count)
            values = returned[where].reshape(count * HALF, 2 * LANES)
            high, low = split(values)
            out = dot(high, lane_inv_v[0]) + dot(low, lane_inv_v[0]) + dot(high, lane_inv_v[1])
            result[where] = out.reshape(count, HALF, 2 * LANES)

        from_planes(base, MINE)
        second_copy.wait()
        from_planes(9 * (1 - core), 8)

        live = jnp.where(slot < count_s[0], 1.0, 0.0).astype(f32)

        def inverse_group(group, carry):
            rows = pl.ds(pl.multiple_of(16 * group, 16), 16)
            re, im = [], []
            for k in range(ROWS):
                value_re = result[k, rows, :LANES]
                if k == 0:
                    re.append(value_re)
                    im.append(None)
                    continue
                value_im = result[k, rows, LANES:]
                c, s = twiddles_v[k, 0:1], twiddles_v[k, 1:2]
                re.append(value_re * c + value_im * s)
                im.append(None if k == ROWS - 1 else value_im * c - value_re * s)
            potential = real_inverse(re, im)
            for column in range(HALF):
                lanes = pl.ds(LANES * column, LANES)
                value = potential[column] * live
                own_terms[slot, rows, lanes] = value * visiting[slot, rows, lanes].astype(f32)
                back_terms[slot, rows, lanes] = value * orb[mine, rows, lanes].astype(f32)
            return carry

        lax.fori_loop(0, 2, inverse_group, 0)
        own_copy(slot).start()

        target = second_s[0, slot]

        def message(piece, carry):
            lanes = pl.ds(pl.multiple_of(512 * piece, 512), 512)

            def earlier(other, total):
                same = jnp.where(second_s[0, other] == target, 1.0, 0.0).astype(f32)
                return total + same * back_terms[other, :, lanes]

            total = lax.fori_loop(0, slot, earlier, back_terms[slot, :, lanes])
            back_rows[slot, :, lanes] = total.astype(bf16)
            return carry

        lax.fori_loop(0, 8, message, 0)
        back_copy(slot).start()
        return carry

    lax.fori_loop(0, slots, one_slot, 0)
    for slot in range(slots):
        visit_copy(slot).wait_send()
        own_copy(slot).wait()
        back_copy(slot).wait()


def exchange(orbitals, pair_first, pair_second, pair_count):
    blocks = lax.axis_size("blk")
    slots = pair_first.shape[1]
    block, rows, cells = orbitals.shape
    lane_fwd, lane_inv = lane_tables()
    row_fwd, row_inv = row_tables()
    tables = [jnp.asarray(t) for t in (lane_fwd, lane_inv, row_fwd, row_inv, filter_table(), twiddle_table())]
    anywhere, vmem, smem = (pl.BlockSpec(memory_space=space) for space in (pl.ANY, pltpu.VMEM, pltpu.SMEM))
    dma, dmas = pltpu.SemaphoreType.DMA, lambda *shape: pltpu.SemaphoreType.DMA(shape)
    return pl.pallas_call(
        functools.partial(pair_kernel, blocks, slots),
        out_shape=[
            jax.ShapeDtypeStruct((slots, rows, cells), f32),
            jax.ShapeDtypeStruct((slots, rows, cells), bf16),
            jax.ShapeDtypeStruct(pair_second.shape, jnp.int32),
            jax.ShapeDtypeStruct(pair_count.shape, jnp.int32),
        ],
        in_specs=[anywhere] * 3 + [smem] * 3 + [anywhere] * len(tables),
        out_specs=[anywhere, anywhere, smem, smem],
        scratch_shapes=[
            pltpu.VMEM((block, rows, cells), bf16),
            pltpu.VMEM((slots, rows, cells), bf16),
            pltpu.VMEM((slots, rows, cells), bf16),
            pltpu.VMEM((slots, rows, cells), f32),
            pltpu.VMEM((slots, rows, cells), f32),
            pltpu.VMEM((slots, rows, cells), bf16),
            pltpu.VMEM((ROWS, HALF, 2 * LANES), bf16),
            pltpu.VMEM((ROWS, HALF, 2 * LANES), bf16),
            pltpu.VMEM((ROWS, HALF, 2 * LANES), f32),
            pltpu.VMEM((MINE, HALF, 2 * LANES), f32),
            pltpu.VMEM((MINE, HALF, 2 * LANES), f32),
            pltpu.VMEM((ROWS, HALF, 2 * LANES), f32),
            pltpu.VMEM((ROWS, HALF, 2 * LANES), f32),
            pltpu.VMEM(lane_fwd.shape, bf16),
            pltpu.VMEM(lane_inv.shape, bf16),
            pltpu.VMEM(row_fwd.shape[1:], bf16),
            pltpu.VMEM(row_inv.shape[1:], bf16),
            pltpu.VMEM((MINE, L, LANES), f32),
            pltpu.VMEM((ROWS, 2, LANES), f32),
            dma, dmas(6), dmas(2), dmas(2), dmas(slots), dmas(slots),
            dmas(slots), dmas(slots), dmas(slots), dma, dma, dma, dma,
        ],
        compiler_params=pltpu.CompilerParams(
            collective_id=0, has_side_effects=True, vmem_limit_bytes=56 * 2**20
        ),
        name="pair_exchange",
    )(orbitals, pair_second, pair_count, pair_first, pair_second, pair_count, *tables)


def merge_kernel(
    slots, block, own_in, back_in, first, count, second, second_count,
    out, own, back, zero, staged, own_sem, back_sem, out_sem,
):
    loads = [pltpu.make_async_copy(own_in, own, own_sem), pltpu.make_async_copy(back_in, back, back_sem)]
    for load in loads:
        load.start()
    zero[...] = jnp.zeros_like(zero)

    def own_live(slot):
        return slot < count[0]

    def back_live(slot):
        return slot < second_count[0]

    for row in range(block):
        touched = jnp.bool_(False)
        for slot in range(slots):
            touched |= own_live(slot) & (first[0, slot] == row)
            touched |= back_live(slot) & (second[0, slot] == row)

        @pl.when(jnp.logical_not(touched))
        def _():
            pltpu.make_async_copy(zero, out.at[row], out_sem).start()

    for load in loads:
        load.wait()

    for slot in range(slots):
        row = first[0, slot]
        seen = jnp.bool_(False)
        for earlier in range(slot):
            seen |= first[0, earlier] == row

        @pl.when(own_live(slot) & jnp.logical_not(seen))
        def _():
            for later in range(slot + 1, slots):

                @pl.when(own_live(later) & (first[0, later] == row))
                def _():
                    own[slot] += own[later]

            for other in range(slots):
                last = back_live(other) & (second[0, other] == row)
                for later in range(other + 1, slots):
                    last &= jnp.logical_not(back_live(later) & (second[0, later] == row))

                @pl.when(last)
                def _():
                    own[slot] += back[other].astype(f32)

            staged[slot] = own[slot].astype(bf16)
            pltpu.make_async_copy(staged.at[slot], out.at[row], out_sem).start()

    for slot in range(slots):
        row = second[0, slot]
        alone = back_live(slot)
        for later in range(slot + 1, slots):
            alone &= jnp.logical_not(back_live(later) & (second[0, later] == row))
        for other in range(slots):
            alone &= jnp.logical_not(own_live(other) & (first[0, other] == row))

        @pl.when(alone)
        def _():
            pltpu.make_async_copy(back.at[slot], out.at[row], out_sem).start()

    pltpu.make_async_copy(out, out, out_sem).wait()


def merge(own, back, pair_first, pair_count, next_second, next_count, shape):
    slots, rows, cells = own.shape
    anywhere, smem = (pl.BlockSpec(memory_space=space) for space in (pl.ANY, pltpu.SMEM))
    return pl.pallas_call(
        functools.partial(merge_kernel, slots, shape[0]),
        out_shape=jax.ShapeDtypeStruct(shape, bf16),
        in_specs=[anywhere] * 2 + [smem] * 4,
        out_specs=anywhere,
        scratch_shapes=[
            pltpu.VMEM((slots, rows, cells), f32),
            pltpu.VMEM((slots, rows, cells), bf16),
            pltpu.VMEM((rows, cells), bf16),
            pltpu.VMEM((slots, rows, cells), bf16),
            pltpu.SemaphoreType.DMA,
            pltpu.SemaphoreType.DMA,
            pltpu.SemaphoreType.DMA,
        ],
        compiler_params=pltpu.CompilerParams(vmem_limit_bytes=32 * 2**20),
        name="merge_rows",
    )(own, back, pair_first, pair_count, next_second, next_count)


def per_device(orbitals, pair_first, pair_second, pair_count):
    own, back, next_second, next_count = exchange(orbitals, pair_first, pair_second, pair_count)
    return merge(own, back, pair_first, pair_count, next_second, next_count, orbitals.shape)


def solution(mesh):
    return jax.shard_map(
        per_device,
        mesh=mesh,
        in_specs=(P("blk", "grid", None), P("blk", None), P("blk", None), P("blk")),
        out_specs=P("blk", "grid", None),
        check_vma=False,
    )
```

time: 669 us -> 72 us (0.11)
  waiting for transfers between devices: 367 us -> 0 us
  local copies, waits for them, and re-layouts: 135 us -> 3.47 us
  Pallas kernels: 0 us -> 67.1 us
  other arithmetic: 55.5 us -> 0 us
  matrix products: 53.8 us -> 0 us
  loops' own time: 18.4 us -> 0 us
  blocking collectives: 18.3 us -> 0 us
  starting transfers between devices: 17.7 us -> 0 us
    ppermute x2 -> x0, waiting for transfers between devices: 367 us -> none  [from_behind(): return lax.ppermute(value, axis, pairs)]
    scatter-add x8 -> x0, local copies, waits for them, and re-layouts: 86.7 us -> none  [the longest x4 43.4 us: slot_step(): totals[0].at[firsts].add(own_slot)]
    pallas_call x0 -> x2, Pallas kernels: none -> 67.1 us  [the longest x1 62.4 us: exchange(): pl.pallas_call(functools.partial(pair_kernel, blocks, slots), out_shape=[...]
    dot_general x40 -> x0, matrix products: 53.8 us -> none  [the longest x16 27.5 us: transform_axis(): jnp.einsum(pattern, tables[1], rotate_parts(values), precision=highest)]
    another operation x8 -> x0, other arithmetic: 27.4 us -> none
    another operation x1 -> x0, loops' own time: 18.4 us -> none  [per_device(): lax.fori_loop(0, turn_count, slot_step, (own_empty, back_empty))]
    all_to_all x4 -> x0, blocking collectives: 18.3 us -> none  [transform_slot(): lax.all_to_all(values, 'grid', split_axis=2, concat_axis=1, tiled=True)]
    another operation x6 -> x0, local copies, waits for them, and re-layouts: 15.3 us -> none
  transfers between devices with their start and end apart: 6 -> 0, of which waited for: 2 -> 0; matrix products, arithmetic and copies ran while one was open for 2% -> 0% of each run, Pallas kernels for 0% -> 0%
where the time goes in v1:
time: 72 us; the launch traced here: 71.3 us
  Pallas kernels  67.1 us (93%)
  local copies, waits for them, and re-layouts  3.47 us (5%)
    pallas_call x1, Pallas kernels, exchange(): pl.pallas_call(functools.partial(pair_kernel, blocks, slots), out_shape=[...  62.4 us
    pallas_call x1, Pallas kernels, merge(): pl.pallas_call(functools.partial(merge_kernel, slots, shape[0]), out_shap...  4.72 us
    unnamed x8, local copies, waits for them, and re-layouts  3.47 us

profile of v1, /device:TPU:0, one launch (start us, length us, event | category | flops | bytes accessed | tf_op | source)
XLA Modules:
  0.0 71.3 jit_solution(17110714163958545104)
XLA Ops:
  0.0 0.0 copy-start.2
  0.7 62.4 %pair_exchange.1 = (f32[4,32,4096]{2,1,0:T(8,128)}, bf16[4,32,4096]{2,1,0:T(8,128)(2,1)}, s32[1,4]{1,0:T(1,128)}, s32[1]{0:T(128)}) custom-call(bf16[32,32,4096]{2,1,0:T(8,128)(2,1)} %orbitals.1, s32[1,4]{1,0:T(1,128)} %second_s.1, s32[1]{0:T(128)S(6)} %copy.11.count_in.count_s.count, s32[1,4]{1,0:T(1,128)} %first.1, s32[1,4]{1,0:T(1,128)} %second_s.1, ...), custom_call_target="tpu_custom_call" | custom-call | tf_op jit(solution)/shard_map/pair_exchange/pallas_call | solution.py:325
  63.0 0.0 copy-done.2
  63.1 0.0 copy-start
  63.1 1.6 %copy-done = f32[4,32,4096]{2,1,0:T(8,128)S(1)} copy-done((f32[4,32,4096]{2,1,0:T(8,128)S(1)}, f32[4,32,4096]{2,1,0:T(8,128)}, u32[]{:S(2)}) %copy-start) | copy-done | bytes 2097176
  64.7 0.0 copy-start.1
  64.7 1.2 %copy-done.1 = bf16[4,32,4096]{2,1,0:T(8,128)(2,1)S(1)} copy-done((bf16[4,32,4096]{2,1,0:T(8,128)(2,1)S(1)}, bf16[4,32,4096]{2,1,0:T(8,128)(2,1)}, u32[]{:S(2)}) %copy-start.1) | copy-done | bytes 1048600
  65.9 0.0 copy-start.3
  65.9 0.7 copy-done.3
  66.5 4.7 %merge_rows.1 = bf16[32,32,4096]{2,1,0:T(8,128)(2,1)} custom-call(f32[4,32,4096]{2,1,0:T(8,128)S(1)} %copy-done, bf16[4,32,4096]{2,1,0:T(8,128)(2,1)S(1)} %copy-done.1, s32[1,4]{1,0:T(1,128)S(1)} %copy-done.2, s32[1]{0:T(128)S(6)} %copy.11.count_in.count_s.count, s32[1,4]{1,0:T(1,128)S(1)} %copy-done.3, s32[1]{0:T(128)} %get-tuple-element.12.second_count), custom_call_target="tpu_custom_call" | custom-call | tf_op jit(solution)/shard_map/merge_rows/pallas_call | solution.py:437
Async XLA Ops:
  0.0 63.0 %copy-start.2 = (s32[1,4]{1,0:T(1,128)S(1)}, s32[1,4]{1,0:T(1,128)}, u32[]{:S(2)}) copy-start(s32[1,4]{1,0:T(1,128)} %first.1) | copy-start | bytes 52
  63.1 1.6 %copy-start = (f32[4,32,4096]{2,1,0:T(8,128)S(1)}, f32[4,32,4096]{2,1,0:T(8,128)}, u32[]{:S(2)}) copy-start(f32[4,32,4096]{2,1,0:T(8,128)} %get-tuple-element.9.own_in) | copy-start | bytes 6291460
  64.7 1.2 %copy-start.1 = (bf16[4,32,4096]{2,1,0:T(8,128)(2,1)S(1)}, bf16[4,32,4096]{2,1,0:T(8,128)(2,1)}, u32[]{:S(2)}) copy-start(bf16[4,32,4096]{2,1,0:T(8,128)(2,1)} %get-tuple-element.10.back_in) | copy-start | bytes 3145732
  65.9 0.7 copy-start.3

commit v2 on v1

--- a/solution.py
+++ b/solution.py
@@ -125,12 +125,12 @@
 
 def pair_kernel(
     blocks, slots,
-    orbitals, second_in, count_in, first_s, second_s, count_s,
+    orbitals, first_in, second_in, count_in,
     lane_fwd, lane_inv, row_fwd, row_inv, filters, twiddles,
     own_out, back_out, next_second, next_count,
     orb, sending, visiting, own_terms, back_terms, back_rows,
     spectra_hi, spectra_lo, planes, others, filtered, returned, result,
-    lane_fwd_v, lane_inv_v, row_fwd_v, row_inv_v, filters_v, twiddles_v,
+    lane_fwd_v, lane_inv_v, row_fwd_v, row_inv_v, filters_v, twiddles_v, first_s, second_s, count_s,
     load_sem, table_sem, index_send, index_recv, visit_send, visit_recv,
     back_send, back_recv, own_sem, first_send, first_recv, second_send, second_recv,
 ):
@@ -147,6 +147,7 @@
             (lane_fwd, lane_fwd_v), (lane_inv, lane_inv_v),
             (row_fwd.at[core], row_fwd_v), (row_inv.at[core], row_inv_v),
             (filters.at[pl.ds(base, MINE)], filters_v), (twiddles, twiddles_v),
+            (first_in, first_s), (second_in, second_s), (count_in, count_s),
         ])
     ]
     for table in tables:
@@ -249,7 +250,7 @@
             filtered[k] = whole[HALF:]
             return carry
 
-        lax.fori_loop(0, MINE, solve, 0)
+        lax.fori_loop(0, MINE, solve, 0, unroll=True)
         second_copy.start()
 
         def from_planes(start, count):
@@ -320,7 +321,7 @@
     lane_fwd, lane_inv = lane_tables()
     row_fwd, row_inv = row_tables()
     tables = [jnp.asarray(t) for t in (lane_fwd, lane_inv, row_fwd, row_inv, filter_table(), twiddle_table())]
-    anywhere, vmem, smem = (pl.BlockSpec(memory_space=space) for space in (pl.ANY, pltpu.VMEM, pltpu.SMEM))
+    anywhere, smem = (pl.BlockSpec(memory_space=space) for space in (pl.ANY, pltpu.SMEM))
     dma, dmas = pltpu.SemaphoreType.DMA, lambda *shape: pltpu.SemaphoreType.DMA(shape)
     return pl.pallas_call(
         functools.partial(pair_kernel, blocks, slots),
@@ -330,7 +331,7 @@
             jax.ShapeDtypeStruct(pair_second.shape, jnp.int32),
             jax.ShapeDtypeStruct(pair_count.shape, jnp.int32),
         ],
-        in_specs=[anywhere] * 3 + [smem] * 3 + [anywhere] * len(tables),
+        in_specs=[anywhere] * (4 + len(tables)),
         out_specs=[anywhere, anywhere, smem, smem],
         scratch_shapes=[
             pltpu.VMEM((block, rows, cells), bf16),
@@ -352,14 +353,17 @@
             pltpu.VMEM(row_inv.shape[1:], bf16),
             pltpu.VMEM((MINE, L, LANES), f32),
             pltpu.VMEM((ROWS, 2, LANES), f32),
-            dma, dmas(6), dmas(2), dmas(2), dmas(slots), dmas(slots),
+            pltpu.SMEM(pair_first.shape, jnp.int32),
+            pltpu.SMEM(pair_second.shape, jnp.int32),
+            pltpu.SMEM(pair_count.shape, jnp.int32),
+            dma, dmas(9), dmas(2), dmas(2), dmas(slots), dmas(slots),
             dmas(slots), dmas(slots), dmas(slots), dma, dma, dma, dma,
         ],
         compiler_params=pltpu.CompilerParams(
-            collective_id=0, has_side_effects=True, vmem_limit_bytes=56 * 2**20
+            collective_id=0, has_side_effects=True, vmem_limit_bytes=60 * 2**20
         ),
         name="pair_exchange",
-    )(orbitals, pair_second, pair_count, pair_first, pair_second, pair_count, *tables)
+    )(orbitals, pair_first, pair_second, pair_count, *tables)
 
 
 def merge_kernel(
@@ -448,7 +452,7 @@
             pltpu.SemaphoreType.DMA,
             pltpu.SemaphoreType.DMA,
         ],
-        compiler_params=pltpu.CompilerParams(vmem_limit_bytes=32 * 2**20),
+        compiler_params=pltpu.CompilerParams(vmem_limit_bytes=60 * 2**20),
         name="merge_rows",
     )(own, back, pair_first, pair_count, next_second, next_count)
 

time: 72 us -> 62.3 us (0.87)
  Pallas kernels: 67.1 us -> 61 us
  local copies, waits for them, and re-layouts: 3.47 us -> 0 us
    pallas_call x1, Pallas kernels: 62.4 us -> 54.2 us  [exchange(): pl.pallas_call(functools.partial(pair_kernel, blocks, slots), out_shape=[...]
    unnamed x8 -> x0, local copies, waits for them, and re-layouts: 3.47 us -> none
    pallas_call x1, Pallas kernels: 4.72 us -> 6.82 us  [merge(): pl.pallas_call(functools.partial(merge_kernel, slots, shape[0]), out_shap...]
where the time goes in v2:
time: 62.3 us; the launch traced here: 61.7 us
  Pallas kernels  61 us (98%)
  between operations  0.66 us (1%)
    pallas_call x1, Pallas kernels, exchange(): pl.pallas_call(functools.partial(pair_kernel, blocks, slots), out_shape=[...  54.2 us
    pallas_call x1, Pallas kernels, merge(): pl.pallas_call(functools.partial(merge_kernel, slots, shape[0]), out_shap...  6.82 us

profile of v2, /device:TPU:0, one launch (start us, length us, event | category | flops | bytes accessed | tf_op | source)
XLA Modules:
  0.0 61.7 jit_solution(13731725163805053476)
XLA Ops:
  0.7 54.2 %pair_exchange.1 = (f32[4,32,4096]{2,1,0:T(8,128)}, bf16[4,32,4096]{2,1,0:T(8,128)(2,1)}, s32[1,4]{1,0:T(1,128)}, s32[1]{0:T(128)}) custom-call(bf16[32,32,4096]{2,1,0:T(8,128)(2,1)} %orbitals.1, s32[1,4]{1,0:T(1,128)} %first.1, s32[1,4]{1,0:T(1,128)} %second_in.1, s32[1]{0:T(128)S(6)} %copy.11.count_in.count, bf16[2,256,256]{2,1,0:T(8,128)(2,1)} %constant.12.clone.lane_fwd, ...), custom_call_target="tpu_custom_call" | custom-call | tf_op jit(solution)/shard_map/pair_exchange/pallas_call | solution.py:326
  54.9 6.8 %merge_rows.1 = bf16[32,32,4096]{2,1,0:T(8,128)(2,1)} custom-call(f32[4,32,4096]{2,1,0:T(8,128)} %get-tuple-element.9.own_in, bf16[4,32,4096]{2,1,0:T(8,128)(2,1)} %get-tuple-element.10.back_in, s32[1,4]{1,0:T(1,128)} %first.1, s32[1]{0:T(128)S(6)} %copy.11.count_in.count, s32[1,4]{1,0:T(1,128)} %get-tuple-element.11.second, s32[1]{0:T(128)} %get-tuple-element.12.second_count), custom_call_target="tpu_custom_call" | custom-call | tf_op jit(solution)/shard_map/merge_rows/pallas_call | solution.py:441

commit v3 on v2

--- a/solution.py
+++ b/solution.py
@@ -17,6 +17,7 @@
 LANES = 128
 ROWS = 17
 MINE = 9
+CODE = 32767.0
 f32 = jnp.float32
 bf16 = jnp.bfloat16
 
@@ -124,19 +125,24 @@
 
 
 def pair_kernel(
-    blocks, slots,
+    blocks, half,
     orbitals, first_in, second_in, count_in,
     lane_fwd, lane_inv, row_fwd, row_inv, filters, twiddles,
-    own_out, back_out, next_second, next_count,
-    orb, sending, visiting, own_terms, back_terms, back_rows,
+    kept_out, codes_out, scales_out, next_second, next_count,
+    orb, sending, arriving, kept, codes, scales,
     spectra_hi, spectra_lo, planes, others, filtered, returned, result,
     lane_fwd_v, lane_inv_v, row_fwd_v, row_inv_v, filters_v, twiddles_v, first_s, second_s, count_s,
-    load_sem, table_sem, index_send, index_recv, visit_send, visit_recv,
-    back_send, back_recv, own_sem, first_send, first_recv, second_send, second_recv,
+    load_sem, table_sem, index_send, index_recv, orbital_send, orbital_recv,
+    code_send, code_recv, scale_send, scale_recv, kept_sem,
+    first_send, first_recv, second_send, second_recv,
 ):
     me, core = lax.axis_index("blk"), lax.axis_index("grid")
     right, left = lax.rem(me + 1, blocks), lax.rem(me + blocks - 1, blocks)
     to_right, to_left, to_partner = {"blk": right}, {"blk": left}, {"grid": 1 - core}
+
+    barrier = pltpu.get_barrier_semaphore()
+    for device in (to_right, to_left, to_partner):
+        pl.semaphore_signal(barrier, inc=1, device_id=device)
 
     load = pltpu.make_async_copy(orbitals, orb, load_sem)
     load.start()
@@ -144,20 +150,15 @@
     tables = [
         pltpu.make_async_copy(source, target, table_sem.at[place])
         for place, (source, target) in enumerate([
+            (first_in, first_s), (second_in, second_s), (count_in, count_s),
             (lane_fwd, lane_fwd_v), (lane_inv, lane_inv_v),
             (row_fwd.at[core], row_fwd_v), (row_inv.at[core], row_inv_v),
             (filters.at[pl.ds(base, MINE)], filters_v), (twiddles, twiddles_v),
-            (first_in, first_s), (second_in, second_s), (count_in, count_s),
         ])
     ]
     for table in tables:
         table.start()
 
-    barrier = pltpu.get_barrier_semaphore()
-    for device in (to_right, to_left, to_partner):
-        pl.semaphore_signal(barrier, inc=1, device_id=device)
-    pl.semaphore_wait(barrier, 3)
-
     def remote(source, target, send, recv, device):
         return pltpu.make_async_remote_copy(
             src_ref=source, dst_ref=target, send_sem=send, recv_sem=recv, device_id=device
@@ -167,43 +168,57 @@
         remote(second_in, next_second, index_send.at[0], index_recv.at[0], to_left),
         remote(count_in, next_count, index_send.at[1], index_recv.at[1], to_left),
     ]
+    pl.semaphore_wait(barrier, 3)
     for copy in index_copies:
         copy.start()
+    for table in tables[:3]:
+        table.wait()
+    load.wait()
+
+    def orbital_copy(m, device):
+        return remote(sending.at[m], arriving.at[m], orbital_send.at[m], orbital_recv.at[m], device)
+
+    for m in range(half, 2 * half):
+        sending[m] = orb[first_s[0, m]]
+        orbital_copy(m, to_left).start()
     for copy in index_copies:
         copy.wait()
-    load.wait()
-
-    def visit_copy(slot):
-        return remote(sending.at[slot], visiting.at[slot], visit_send.at[slot], visit_recv.at[slot], to_right)
-
-    def back_copy(slot):
-        return remote(back_rows.at[slot], back_out.at[slot], back_send.at[slot], back_recv.at[slot], to_left)
-
-    def own_copy(slot):
-        return pltpu.make_async_copy(own_terms.at[slot], own_out.at[slot], own_sem.at[slot])
-
-    for slot in range(slots):
-        sending[slot] = orb[next_second[0, slot]]
-        visit_copy(slot).start()
-    for table in tables:
+    for m in range(half):
+        sending[m] = orb[next_second[0, m]]
+        orbital_copy(m, to_right).start()
+    for table in tables[3:]:
         table.wait()
 
+    def kept_copy(m):
+        return pltpu.make_async_copy(kept.at[m], kept_out.at[m], kept_sem.at[m])
+
+    def code_copy(m, device):
+        return remote(codes.at[m], codes_out.at[m], code_send.at[m], code_recv.at[m], device)
+
+    def scale_copy(m, device):
+        return remote(scales.at[m], scales_out.at[m], scale_send.at[m], scale_recv.at[m], device)
+
     other_base = 8 * (1 - core)
-    first_copy = remote(planes.at[pl.ds(other_base, MINE)], others, first_send, first_recv, to_partner)
-    second_copy = remote(
-        filtered.at[pl.ds(core, 8)], returned.at[pl.ds(base + core, 8)], second_send, second_recv, to_partner
-    )
-
-    def one_slot(slot, carry):
-        mine = first_s[0, slot]
-        visit_copy(slot).wait_recv()
-
+
+    def first_copy(which):
+        return remote(
+            planes.at[which, pl.ds(other_base, MINE)], others.at[which],
+            first_send.at[which], first_recv.at[which], to_partner,
+        )
+
+    def second_copy(which):
+        return remote(
+            filtered.at[which, pl.ds(core, 8)], returned.at[which, pl.ds(base + core, 8)],
+            second_send.at[which], second_recv.at[which], to_partner,
+        )
+
+    def forward(which, left_part, right_part):
         def forward_group(group, carry):
             rows = pl.ds(pl.multiple_of(16 * group, 16), 16)
             values = []
             for column in range(HALF):
                 lanes = pl.ds(LANES * column, LANES)
-                values.append(orb[mine, rows, lanes].astype(f32) * visiting[slot, rows, lanes].astype(f32))
+                values.append(left_part(rows, lanes).astype(f32) * right_part(rows, lanes).astype(f32))
             re, im = real_forward(values)
             for k in range(ROWS):
                 if k == 0:
@@ -227,15 +242,16 @@
             high = spectra_hi[where].reshape(count * HALF, 2 * LANES)
             low = spectra_lo[where].reshape(count * HALF, 2 * LANES)
             out = dot(high, lane_fwd_v[0]) + dot(low, lane_fwd_v[0]) + dot(high, lane_fwd_v[1])
-            planes[where] = out.reshape(count, HALF, 2 * LANES)
+            planes[which, where] = out.reshape(count, HALF, 2 * LANES)
 
         to_planes(other_base, MINE)
-        first_copy.start()
+        first_copy(which).start()
         to_planes(base + core, 8)
-        first_copy.wait()
-
-        def solve(k, carry):
-            values = jnp.concatenate([planes[base + k], others[k]], 0)
+
+    def solve(which):
+        first_copy(which).wait()
+        for k in range(MINE):
+            values = jnp.concatenate([planes[which, base + k], others[which, k]], 0)
             high, low = split(values)
             out = dot(row_fwd_v[...], jnp.concatenate([high, low, high], 0))
             kernel = filters_v[k]
@@ -246,25 +262,21 @@
             re = out[:L, :LANES] - out[L:, LANES:]
             im = out[:L, LANES:] + out[L:, :LANES]
             whole = jnp.concatenate([re, im], 1)
-            returned[base + k] = whole[:HALF]
-            filtered[k] = whole[HALF:]
-            return carry
-
-        lax.fori_loop(0, MINE, solve, 0, unroll=True)
-        second_copy.start()
-
+            returned[which, base + k] = whole[:HALF]
+            filtered[which, k] = whole[HALF:]
+        second_copy(which).start()
+
+    def inverse(which, m, live, here, came):
         def from_planes(start, count):
             where = pl.ds(start, count)
-            values = returned[where].reshape(count * HALF, 2 * LANES)
+            values = returned[which, where].reshape(count * HALF, 2 * LANES)
             high, low = split(values)
             out = dot(high, lane_inv_v[0]) + dot(low, lane_inv_v[0]) + dot(high, lane_inv_v[1])
             result[where] = out.reshape(count, HALF, 2 * LANES)
 
         from_planes(base, MINE)
-        second_copy.wait()
+        second_copy(which).wait()
         from_planes(9 * (1 - core), 8)
-
-        live = jnp.where(slot < count_s[0], 1.0, 0.0).astype(f32)
 
         def inverse_group(group, carry):
             rows = pl.ds(pl.multiple_of(16 * group, 16), 16)
@@ -280,38 +292,52 @@
                 re.append(value_re * c + value_im * s)
                 im.append(None if k == ROWS - 1 else value_im * c - value_re * s)
             potential = real_inverse(re, im)
+            terms, largest = [], None
             for column in range(HALF):
                 lanes = pl.ds(LANES * column, LANES)
                 value = potential[column] * live
-                own_terms[slot, rows, lanes] = value * visiting[slot, rows, lanes].astype(f32)
-                back_terms[slot, rows, lanes] = value * orb[mine, rows, lanes].astype(f32)
+                kept[m, rows, lanes] = value * came(rows, lanes).astype(f32)
+                terms.append(value * here(rows, lanes).astype(f32))
+                size = jnp.abs(terms[-1])
+                largest = size if largest is None else jnp.maximum(largest, size)
+            bound = jnp.maximum(jnp.max(largest, axis=1, keepdims=True), 1e-30)
+            scales[m, rows, :] = jnp.broadcast_to(bound * (1.0 / CODE), (16, LANES))
+            inverse_scale = CODE / bound
+            for column in range(HALF):
+                lanes = pl.ds(LANES * column, LANES)
+                code = jnp.round(terms[column] * inverse_scale)
+                codes[m, rows, lanes] = code.astype(jnp.int32).astype(jnp.int16)
             return carry
 
         lax.fori_loop(0, 2, inverse_group, 0)
-        own_copy(slot).start()
-
-        target = second_s[0, slot]
-
-        def message(piece, carry):
-            lanes = pl.ds(pl.multiple_of(512 * piece, 512), 512)
-
-            def earlier(other, total):
-                same = jnp.where(second_s[0, other] == target, 1.0, 0.0).astype(f32)
-                return total + same * back_terms[other, :, lanes]
-
-            total = lax.fori_loop(0, slot, earlier, back_terms[slot, :, lanes])
-            back_rows[slot, :, lanes] = total.astype(bf16)
-            return carry
-
-        lax.fori_loop(0, 8, message, 0)
-        back_copy(slot).start()
+        kept_copy(m).start()
+
+    def one_stage(stage, carry):
+        mine, second = first_s[0, stage], next_second[0, half + stage]
+        pairs = (
+            (lambda rows, lanes: orb[mine, rows, lanes], lambda rows, lanes: arriving[stage, rows, lanes]),
+            (lambda rows, lanes: orb[second, rows, lanes], lambda rows, lanes: arriving[half + stage, rows, lanes]),
+        )
+        orbital_copy(half + stage, to_left).wait_recv()
+        forward(1, *pairs[1])
+        orbital_copy(stage, to_right).wait_recv()
+        forward(0, *pairs[0])
+        solve(1)
+        solve(0)
+        inverse(1, half + stage, jnp.where(half + stage < next_count[0], 1.0, 0.0).astype(f32), *pairs[1])
+        code_copy(half + stage, to_right).start()
+        scale_copy(half + stage, to_right).start()
+        inverse(0, stage, jnp.where(stage < count_s[0], 1.0, 0.0).astype(f32), *pairs[0])
+        code_copy(stage, to_left).start()
+        scale_copy(stage, to_left).start()
         return carry
 
-    lax.fori_loop(0, slots, one_slot, 0)
-    for slot in range(slots):
-        visit_copy(slot).wait_send()
-        own_copy(slot).wait()
-        back_copy(slot).wait()
+    lax.fori_loop(0, half, one_stage, 0)
+    for m in range(2 * half):
+        orbital_copy(m, to_left).wait_send()
+        kept_copy(m).wait()
+        code_copy(m, to_left).wait()
+        scale_copy(m, to_left).wait()
 
 
 def exchange(orbitals, pair_first, pair_second, pair_count):
@@ -324,28 +350,29 @@
     anywhere, smem = (pl.BlockSpec(memory_space=space) for space in (pl.ANY, pltpu.SMEM))
     dma, dmas = pltpu.SemaphoreType.DMA, lambda *shape: pltpu.SemaphoreType.DMA(shape)
     return pl.pallas_call(
-        functools.partial(pair_kernel, blocks, slots),
+        functools.partial(pair_kernel, blocks, slots // 2),
         out_shape=[
             jax.ShapeDtypeStruct((slots, rows, cells), f32),
-            jax.ShapeDtypeStruct((slots, rows, cells), bf16),
+            jax.ShapeDtypeStruct((slots, rows, cells), jnp.int16),
+            jax.ShapeDtypeStruct((slots, rows, LANES), f32),
             jax.ShapeDtypeStruct(pair_second.shape, jnp.int32),
             jax.ShapeDtypeStruct(pair_count.shape, jnp.int32),
         ],
         in_specs=[anywhere] * (4 + len(tables)),
-        out_specs=[anywhere, anywhere, smem, smem],
+        out_specs=[anywhere, anywhere, anywhere, smem, smem],
         scratch_shapes=[
             pltpu.VMEM((block, rows, cells), bf16),
             pltpu.VMEM((slots, rows, cells), bf16),
             pltpu.VMEM((slots, rows, cells), bf16),
             pltpu.VMEM((slots, rows, cells), f32),
-            pltpu.VMEM((slots, rows, cells), f32),
-            pltpu.VMEM((slots, rows, cells), bf16),
+            pltpu.VMEM((slots, rows, cells), jnp.int16),
+            pltpu.VMEM((slots, rows, LANES), f32),
             pltpu.VMEM((ROWS, HALF, 2 * LANES), bf16),
             pltpu.VMEM((ROWS, HALF, 2 * LANES), bf16),
-            pltpu.VMEM((ROWS, HALF, 2 * LANES), f32),
-            pltpu.VMEM((MINE, HALF, 2 * LANES), f32),
-            pltpu.VMEM((MINE, HALF, 2 * LANES), f32),
-            pltpu.VMEM((ROWS, HALF, 2 * LANES), f32),
+            pltpu.VMEM((2, ROWS, HALF, 2 * LANES), f32),
+            pltpu.VMEM((2, MINE, HALF, 2 * LANES), f32),
+            pltpu.VMEM((2, MINE, HALF, 2 * LANES), f32),
+            pltpu.VMEM((2, ROWS, HALF, 2 * LANES), f32),
             pltpu.VMEM((ROWS, HALF, 2 * LANES), f32),
             pltpu.VMEM(lane_fwd.shape, bf16),
             pltpu.VMEM(lane_inv.shape, bf16),
@@ -357,7 +384,8 @@
             pltpu.SMEM(pair_second.shape, jnp.int32),
             pltpu.SMEM(pair_count.shape, jnp.int32),
             dma, dmas(9), dmas(2), dmas(2), dmas(slots), dmas(slots),
-            dmas(slots), dmas(slots), dmas(slots), dma, dma, dma, dma,
+            dmas(slots), dmas(slots), dmas(slots), dmas(slots), dmas(slots),
+            dmas(2), dmas(2), dmas(2), dmas(2),
         ],
         compiler_params=pltpu.CompilerParams(
             collective_id=0, has_side_effects=True, vmem_limit_bytes=60 * 2**20
@@ -367,19 +395,27 @@
 
 
 def merge_kernel(
-    slots, block, own_in, back_in, first, count, second, second_count,
-    out, own, back, zero, staged, own_sem, back_sem, out_sem,
+    half, block, kept_in, codes_in, scales_in, first, count, second, second_count,
+    out, kept, codes, scales, total, zero, staged, kept_sem, code_sem, scale_sem, out_sem,
 ):
-    loads = [pltpu.make_async_copy(own_in, own, own_sem), pltpu.make_async_copy(back_in, back, back_sem)]
-    for load in loads:
-        load.start()
-    zero[...] = jnp.zeros_like(zero)
+    slots = 2 * half
+    pieces, width = 8, zero.shape[1] // 8
 
     def own_live(slot):
         return slot < count[0]
 
     def back_live(slot):
         return slot < second_count[0]
+
+    loads = []
+    for m in range(slots):
+        kept_live, code_live = (own_live(m), back_live(m)) if m < half else (back_live(m), own_live(m))
+        loads.append((kept_live, pltpu.make_async_copy(kept_in.at[m], kept.at[m], kept_sem.at[m])))
+        loads.append((code_live, pltpu.make_async_copy(codes_in.at[m], codes.at[m], code_sem.at[m])))
+        loads.append((code_live, pltpu.make_async_copy(scales_in.at[m], scales.at[m], scale_sem.at[m])))
+    for needed, load in loads:
+        pl.when(needed)(load.start)
+    zero[...] = jnp.zeros_like(zero)
 
     for row in range(block):
         touched = jnp.bool_(False)
@@ -391,75 +427,122 @@
         def _():
             pltpu.make_async_copy(zero, out.at[row], out_sem).start()
 
-    for load in loads:
-        load.wait()
-
+    for needed, load in loads:
+        pl.when(needed)(load.wait)
+
+    def over_pieces(body):
+        def piece(index, carry):
+            body(pl.ds(pl.multiple_of(width * index, width), width))
+            return carry
+
+        lax.fori_loop(0, pieces, piece, 0)
+
+    def term(is_kept, m, lanes):
+        if is_kept:
+            return kept[m, :, lanes]
+        return codes[m, :, lanes].astype(f32) * scales[m, :, 0:1]
+
+    def add_up(place, kind_half, lead, live, rows, extra):
+        several = jnp.bool_(False)
+        for later in range(lead + 1, slots):
+            several |= live(later) & (rows[0, later] == rows[0, lead])
+        for flag, other in extra:
+            several |= flag
+
+        @pl.when(jnp.logical_not(several))
+        def _():
+            def only(lanes):
+                staged[place, :, lanes] = term(kind_half(lead), lead, lanes).astype(bf16)
+
+            over_pieces(only)
+
+        @pl.when(several)
+        def _():
+            def begin(lanes):
+                total[:, lanes] = term(kind_half(lead), lead, lanes)
+
+            over_pieces(begin)
+            for later in range(lead + 1, slots):
+
+                @pl.when(live(later) & (rows[0, later] == rows[0, lead]))
+                def _():
+                    def more(lanes):
+                        total[:, lanes] += term(kind_half(later), later, lanes)
+
+                    over_pieces(more)
+
+            for flag, other in extra:
+
+                @pl.when(flag)
+                def _():
+                    def more(lanes):
+                        total[:, lanes] += staged[other, :, lanes].astype(f32)
+
+                    over_pieces(more)
+
+            def end(lanes):
+                staged[place, :, lanes] = total[:, lanes].astype(bf16)
+
+            over_pieces(end)
+
+    leads = []
     for slot in range(slots):
-        row = first[0, slot]
-        seen = jnp.bool_(False)
+        lead = back_live(slot)
         for earlier in range(slot):
-            seen |= first[0, earlier] == row
-
-        @pl.when(own_live(slot) & jnp.logical_not(seen))
+            lead &= second[0, earlier] != second[0, slot]
+        leads.append(lead)
+
+        @pl.when(lead)
         def _():
-            for later in range(slot + 1, slots):
-
-                @pl.when(own_live(later) & (first[0, later] == row))
-                def _():
-                    own[slot] += own[later]
-
+            add_up(slot, lambda s: s >= half, slot, back_live, second, [])
+            owned = jnp.bool_(False)
             for other in range(slots):
-                last = back_live(other) & (second[0, other] == row)
-                for later in range(other + 1, slots):
-                    last &= jnp.logical_not(back_live(later) & (second[0, later] == row))
-
-                @pl.when(last)
-                def _():
-                    own[slot] += back[other].astype(f32)
-
-            staged[slot] = own[slot].astype(bf16)
-            pltpu.make_async_copy(staged.at[slot], out.at[row], out_sem).start()
+                owned |= own_live(other) & (first[0, other] == second[0, slot])
+
+            @pl.when(jnp.logical_not(owned))
+            def _():
+                pltpu.make_async_copy(staged.at[slot], out.at[second[0, slot]], out_sem).start()
 
     for slot in range(slots):
-        row = second[0, slot]
-        alone = back_live(slot)
-        for later in range(slot + 1, slots):
-            alone &= jnp.logical_not(back_live(later) & (second[0, later] == row))
-        for other in range(slots):
-            alone &= jnp.logical_not(own_live(other) & (first[0, other] == row))
-
-        @pl.when(alone)
+        lead = own_live(slot)
+        for earlier in range(slot):
+            lead &= first[0, earlier] != first[0, slot]
+
+        @pl.when(lead)
         def _():
-            pltpu.make_async_copy(back.at[slot], out.at[row], out_sem).start()
+            extra = [(leads[other] & (second[0, other] == first[0, slot]), other) for other in range(slots)]
+            add_up(slots + slot, lambda s: s < half, slot, own_live, first, extra)
+            pltpu.make_async_copy(staged.at[slots + slot], out.at[first[0, slot]], out_sem).start()
 
     pltpu.make_async_copy(out, out, out_sem).wait()
 
 
-def merge(own, back, pair_first, pair_count, next_second, next_count, shape):
-    slots, rows, cells = own.shape
+def merge(kept, codes, scales, pair_first, pair_count, next_second, next_count, shape):
+    slots, rows, cells = kept.shape
     anywhere, smem = (pl.BlockSpec(memory_space=space) for space in (pl.ANY, pltpu.SMEM))
+    dma, dmas = pltpu.SemaphoreType.DMA, pltpu.SemaphoreType.DMA((slots,))
     return pl.pallas_call(
-        functools.partial(merge_kernel, slots, shape[0]),
+        functools.partial(merge_kernel, slots // 2, shape[0]),
         out_shape=jax.ShapeDtypeStruct(shape, bf16),
-        in_specs=[anywhere] * 2 + [smem] * 4,
+        in_specs=[anywhere] * 3 + [smem] * 4,
         out_specs=anywhere,
         scratch_shapes=[
-            pltpu.VMEM((slots, rows, cells), f32),
-            pltpu.VMEM((slots, rows, cells), bf16),
+            pltpu.VMEM(kept.shape, f32),
+            pltpu.VMEM(codes.shape, jnp.int16),
+            pltpu.VMEM(scales.shape, f32),
+            pltpu.VMEM((rows, cells), f32),
             pltpu.VMEM((rows, cells), bf16),
-            pltpu.VMEM((slots, rows, cells), bf16),
-            pltpu.SemaphoreType.DMA,
-            pltpu.SemaphoreType.DMA,
-            pltpu.SemaphoreType.DMA,
+            pltpu.VMEM((2 * slots, rows, cells), bf16),
+            dmas, dmas, dmas, dma,
         ],
         compiler_params=pltpu.CompilerParams(vmem_limit_bytes=60 * 2**20),
         name="merge_rows",
-    )(own, back, pair_first, pair_count, next_second, next_count)
+    )(kept, codes, scales, pair_first, pair_count, next_second, next_count)
 
 
 def per_device(orbitals, pair_first, pair_second, pair_count):
-    own, back, next_second, next_count = exchange(orbitals, pair_first, pair_second, pair_count)
-    return merge(own, back, pair_first, pair_count, next_second, next_count, orbitals.shape)
+    kept, codes, scales, next_second, next_count = exchange(orbitals, pair_first, pair_second, pair_count)
+    return merge(kept, codes, scales, pair_first, pair_count, next_second, next_count, orbitals.shape)
 
 
 def solution(mesh):

time: 62.3 us -> 52.1 us (0.84)
  Pallas kernels: 61 us -> 50.8 us
    pallas_call x2, Pallas kernels: 61 us -> 50.8 us  [the longest x1 44.3 us: exchange(): pl.pallas_call(functools.partial(pair_kernel, blocks, slots // 2), out_sh...]
where the time goes in v3:
time: 52.1 us; the launch traced here: 51.4 us
  Pallas kernels  50.8 us (98%)
  between operations  0.66 us (1%)
    pallas_call x1, Pallas kernels, exchange(): pl.pallas_call(functools.partial(pair_kernel, blocks, slots // 2), out_sh...  44.3 us
    pallas_call x1, Pallas kernels, merge(): pl.pallas_call(functools.partial(merge_kernel, slots // 2, shape[0]), out...  6.43 us

profile of v3, /device:TPU:0, one launch (start us, length us, event | category | flops | bytes accessed | tf_op | source)
XLA Modules:
  0.0 51.4 jit_solution(7362224191334886133)
XLA Ops:
  0.7 44.3 %pair_exchange.1 = (f32[4,32,4096]{2,1,0:T(8,128)}, s16[4,32,4096]{2,1,0:T(8,128)(2,1)}, f32[4,32,128]{2,1,0:T(8,128)}, s32[1,4]{1,0:T(1,128)}, s32[1]{0:T(128)}) custom-call(bf16[32,32,4096]{2,1,0:T(8,128)(2,1)} %orbitals.1, s32[1,4]{1,0:T(1,128)} %first.1, s32[1,4]{1,0:T(1,128)} %second_in.1, s32[1]{0:T(128)S(6)} %copy.11.count_in.count, ...), custom_call_target="tpu_custom_call" | custom-call | tf_op jit(solution)/shard_map/pair_exchange/pallas_call | solution.py:352
  45.0 6.4 %merge_rows.1 = bf16[32,32,4096]{2,1,0:T(8,128)(2,1)} custom-call(f32[4,32,4096]{2,1,0:T(8,128)} %get-tuple-element.10.kept_in, s16[4,32,4096]{2,1,0:T(8,128)(2,1)} %get-tuple-element.11.codes_in, f32[4,32,128]{2,1,0:T(8,128)} %get-tuple-element.12.scales_in, s32[1,4]{1,0:T(1,128)} %first.1, s32[1]{0:T(128)S(6)} %copy.11.count_in.count, ...), custom_call_target="tpu_custom_call" | custom-call | tf_op jit(solution)/shard_map/merge_rows/pallas_call | solution.py:524

commit v4 on v3

--- a/solution.py
+++ b/solution.py
@@ -36,7 +36,8 @@
     imag = np.kron(sign, -np.sin(angle))
     forward = np.block([[real, imag], [-imag, real]])
     inverse = np.block([[real, -imag], [imag, real]])
-    return np.stack(split_table(forward)), np.stack(split_table(inverse))
+    (forward, low), (inverse, inverse_low) = split_table(forward), split_table(inverse)
+    return np.concatenate([forward, forward, low]), np.concatenate([inverse, inverse, inverse_low])
 
 
 def row_tables():
@@ -125,24 +126,36 @@
 
 
 def pair_kernel(
-    blocks, half,
+    blocks, slots,
     orbitals, first_in, second_in, count_in,
     lane_fwd, lane_inv, row_fwd, row_inv, filters, twiddles,
-    kept_out, codes_out, scales_out, next_second, next_count,
+    kept_out, codes_out, scales_out, info,
     orb, sending, arriving, kept, codes, scales,
-    spectra_hi, spectra_lo, planes, others, filtered, returned, result,
+    spectra, planes, others, filtered, returned, result,
     lane_fwd_v, lane_inv_v, row_fwd_v, row_inv_v, filters_v, twiddles_v, first_s, second_s, count_s,
-    load_sem, table_sem, index_send, index_recv, orbital_send, orbital_recv,
+    next_second, next_count, relay_second, relay_count, final_here, relay_send, relay_recv, load_sem, table_sem, index_send, index_recv, orbital_send, orbital_recv,
     code_send, code_recv, scale_send, scale_recv, kept_sem,
     first_send, first_recv, second_send, second_recv,
 ):
+    half = slots // 2
     me, core = lax.axis_index("blk"), lax.axis_index("grid")
     right, left = lax.rem(me + 1, blocks), lax.rem(me + blocks - 1, blocks)
     to_right, to_left, to_partner = {"blk": right}, {"blk": left}, {"grid": 1 - core}
 
+    final, relay = blocks - 1, max(2, blocks // 4) - 1
+    is_first, is_final, is_relay = me == 0, me == final, me == relay
     barrier = pltpu.get_barrier_semaphore()
-    for device in (to_right, to_left, to_partner):
+    for device in (to_left, to_partner):
         pl.semaphore_signal(barrier, inc=1, device_id=device)
+
+    @pl.when(jnp.logical_not(is_final))
+    def _():
+        pl.semaphore_signal(barrier, inc=1, device_id=to_right)
+
+    @pl.when(is_relay)
+    def _():
+        pl.semaphore_signal(barrier, inc=1, device_id={"blk": 0})
+        pl.semaphore_signal(barrier, inc=1, device_id={"blk": final})
 
     load = pltpu.make_async_copy(orbitals, orb, load_sem)
     load.start()
@@ -164,36 +177,99 @@
             src_ref=source, dst_ref=target, send_sem=send, recv_sem=recv, device_id=device
         )
 
-    index_copies = [
-        remote(second_in, next_second, index_send.at[0], index_recv.at[0], to_left),
-        remote(count_in, next_count, index_send.at[1], index_recv.at[1], to_left),
-    ]
-    pl.semaphore_wait(barrier, 3)
-    for copy in index_copies:
-        copy.start()
-    for table in tables[:3]:
-        table.wait()
-    load.wait()
-
-    def orbital_copy(m, device):
-        return remote(sending.at[m], arriving.at[m], orbital_send.at[m], orbital_recv.at[m], device)
-
-    for m in range(half, 2 * half):
-        sending[m] = orb[first_s[0, m]]
-        orbital_copy(m, to_left).start()
-    for copy in index_copies:
-        copy.wait()
-    for m in range(half):
-        sending[m] = orb[next_second[0, m]]
-        orbital_copy(m, to_right).start()
+    def index_copies(targets, sent, arrived, device, sources=(second_in, count_in)):
+        return [
+            remote(source, target, sent.at[part], arrived.at[part], device)
+            for part, (source, target) in enumerate(zip(sources, targets))
+        ]
+
+    to_next = index_copies((next_second, next_count), index_send, index_recv, to_left)
+    to_relay = index_copies((relay_second, relay_count), index_send, relay_recv, {"blk": relay})
+
+    def orbital_copy(m, group, device):
+        part = pl.ds(16 * group, 16)
+        return remote(
+            sending.at[m, part], arriving.at[m, part], orbital_send.at[m, group], orbital_recv.at[m, group], device
+        )
+
+    def send_first(m, device):
+        for group in range(2):
+            orbital_copy(m, group, device).start()
+
+    def load_own():
+        for table in tables[:3]:
+            table.wait()
+        load.wait()
+        for m in range(half, slots):
+            sending[m] = orb[first_s[0, m]]
+
+    def load_visits():
+        for copy in to_next:
+            copy.wait_recv()
+        for m in range(half):
+            sending[m] = orb[next_second[0, m]]
+
+    @pl.when(jnp.logical_not(is_final))
+    def _():
+        pl.semaphore_wait(barrier, 3)
+
+    @pl.when(is_final)
+    def _():
+        pl.semaphore_wait(barrier, 4)
+        pl.semaphore_signal(final_here, inc=1, device_id=to_right)
+        pl.semaphore_signal(final_here, inc=1, device_id={"blk": relay})
+
+    @pl.when(is_first)
+    def _():
+        for copy in to_relay:
+            copy.start()
+        load_own()
+        load_visits()
+        send_first(0, to_right)
+        pl.semaphore_wait(final_here, 1)
+        send_first(half, to_left)
+
+    @pl.when(jnp.logical_not(is_first))
+    def _():
+        for copy in to_next:
+            copy.start()
+        load_own()
+        send_first(half, to_left)
+
+        @pl.when(is_relay)
+        def _():
+            for copy in to_relay:
+                copy.wait_recv()
+            pl.semaphore_wait(final_here, 1)
+            onward = index_copies(
+                (next_second, next_count), relay_send, index_recv, {"blk": final}, (relay_second, relay_count)
+            )
+            for copy in onward:
+                copy.start()
+            for copy in onward:
+                copy.wait_send()
+
+        load_visits()
+        send_first(0, to_right)
+
+    for copy in to_next:
+        copy.wait_send()
+    for stage in range(1, half):
+        for group in range(2):
+            for m, device in ((half + stage, to_left), (stage, to_right)):
+                orbital_copy(m - 1, group, device).wait_send()
+                orbital_copy(m, group, device).start()
     for table in tables[3:]:
         table.wait()
 
     def kept_copy(m):
         return pltpu.make_async_copy(kept.at[m], kept_out.at[m], kept_sem.at[m])
 
-    def code_copy(m, device):
-        return remote(codes.at[m], codes_out.at[m], code_send.at[m], code_recv.at[m], device)
+    def code_copy(m, group, device):
+        part = pl.ds(16 * group, 16)
+        return remote(
+            codes.at[m, part], codes_out.at[m, part], code_send.at[m, group], code_recv.at[m, group], device
+        )
 
     def scale_copy(m, device):
         return remote(scales.at[m], scales_out.at[m], scale_send.at[m], scale_recv.at[m], device)
@@ -212,13 +288,16 @@
             second_send.at[which], second_recv.at[which], to_partner,
         )
 
-    def forward(which, left_part, right_part):
+    def forward(stage, which):
+        m, here = stage + half * which, jnp.where(which == 0, first_s[0, stage], next_second[0, half + stage])
+
         def forward_group(group, carry):
+            orbital_copy(m, group, to_left).wait_recv()
             rows = pl.ds(pl.multiple_of(16 * group, 16), 16)
             values = []
             for column in range(HALF):
                 lanes = pl.ds(LANES * column, LANES)
-                values.append(left_part(rows, lanes).astype(f32) * right_part(rows, lanes).astype(f32))
+                values.append(orb[here, rows, lanes].astype(f32) * arriving[m, rows, lanes].astype(f32))
             re, im = real_forward(values)
             for k in range(ROWS):
                 if k == 0:
@@ -231,24 +310,23 @@
                         turned_re, turned_im = re[k] * c - im[k] * s, re[k] * s + im[k] * c
                 for part, value in enumerate((turned_re, turned_im)):
                     high, low = split(value)
-                    spectra_hi[k, rows, LANES * part : LANES * (part + 1)] = high
-                    spectra_lo[k, rows, LANES * part : LANES * (part + 1)] = low
+                    for place, piece in enumerate((high, low, high)):
+                        start = LANES * (2 * place + part)
+                        spectra[k, rows, start : start + LANES] = piece
             return carry
 
         lax.fori_loop(0, 2, forward_group, 0)
 
         def to_planes(start, count):
             where = pl.ds(start, count)
-            high = spectra_hi[where].reshape(count * HALF, 2 * LANES)
-            low = spectra_lo[where].reshape(count * HALF, 2 * LANES)
-            out = dot(high, lane_fwd_v[0]) + dot(low, lane_fwd_v[0]) + dot(high, lane_fwd_v[1])
+            out = dot(spectra[where].reshape(count * HALF, 6 * LANES), lane_fwd_v[...])
             planes[which, where] = out.reshape(count, HALF, 2 * LANES)
 
         to_planes(other_base, MINE)
         first_copy(which).start()
         to_planes(base + core, 8)
 
-    def solve(which):
+    def solve(stage, which):
         first_copy(which).wait()
         for k in range(MINE):
             values = jnp.concatenate([planes[which, base + k], others[which, k]], 0)
@@ -266,12 +344,16 @@
             filtered[which, k] = whole[HALF:]
         second_copy(which).start()
 
-    def inverse(which, m, live, here, came):
+    def inverse(stage, which):
+        m, here = stage + half * which, jnp.where(which == 0, first_s[0, stage], next_second[0, half + stage])
+        live = jnp.where(m < jnp.where(which == 0, count_s[0], next_count[0]), 1.0, 0.0).astype(f32)
+        device = {"blk": jnp.where(which == 0, left, right)}
+
         def from_planes(start, count):
             where = pl.ds(start, count)
             values = returned[which, where].reshape(count * HALF, 2 * LANES)
             high, low = split(values)
-            out = dot(high, lane_inv_v[0]) + dot(low, lane_inv_v[0]) + dot(high, lane_inv_v[1])
+            out = dot(jnp.concatenate([high, low, high], 1), lane_inv_v[...])
             result[where] = out.reshape(count, HALF, 2 * LANES)
 
         from_planes(base, MINE)
@@ -296,8 +378,8 @@
             for column in range(HALF):
                 lanes = pl.ds(LANES * column, LANES)
                 value = potential[column] * live
-                kept[m, rows, lanes] = value * came(rows, lanes).astype(f32)
-                terms.append(value * here(rows, lanes).astype(f32))
+                kept[m, rows, lanes] = value * arriving[m, rows, lanes].astype(f32)
+                terms.append(value * orb[here, rows, lanes].astype(f32))
                 size = jnp.abs(terms[-1])
                 largest = size if largest is None else jnp.maximum(largest, size)
             bound = jnp.maximum(jnp.max(largest, axis=1, keepdims=True), 1e-30)
@@ -307,37 +389,37 @@
                 lanes = pl.ds(LANES * column, LANES)
                 code = jnp.round(terms[column] * inverse_scale)
                 codes[m, rows, lanes] = code.astype(jnp.int32).astype(jnp.int16)
+            code_copy(m, group, device).start()
             return carry
 
         lax.fori_loop(0, 2, inverse_group, 0)
+        scale_copy(m, device).start()
         kept_copy(m).start()
 
     def one_stage(stage, carry):
-        mine, second = first_s[0, stage], next_second[0, half + stage]
-        pairs = (
-            (lambda rows, lanes: orb[mine, rows, lanes], lambda rows, lanes: arriving[stage, rows, lanes]),
-            (lambda rows, lanes: orb[second, rows, lanes], lambda rows, lanes: arriving[half + stage, rows, lanes]),
-        )
-        orbital_copy(half + stage, to_left).wait_recv()
-        forward(1, *pairs[1])
-        orbital_copy(stage, to_right).wait_recv()
-        forward(0, *pairs[0])
-        solve(1)
-        solve(0)
-        inverse(1, half + stage, jnp.where(half + stage < next_count[0], 1.0, 0.0).astype(f32), *pairs[1])
-        code_copy(half + stage, to_right).start()
-        scale_copy(half + stage, to_right).start()
-        inverse(0, stage, jnp.where(stage < count_s[0], 1.0, 0.0).astype(f32), *pairs[0])
-        code_copy(stage, to_left).start()
-        scale_copy(stage, to_left).start()
+        for phase in (forward, solve, inverse):
+            def one_slot(turn, carry):
+                phase(stage, 1 - turn)
+                return carry
+
+            lax.fori_loop(0, 2, one_slot, 0)
         return carry
 
+    for m in range(slots):
+        info[0, m] = first_s[0, m]
+        info[0, slots + m] = next_second[0, m]
+    info[0, 2 * slots] = count_s[0]
+    info[0, 2 * slots + 1] = next_count[0]
+
     lax.fori_loop(0, half, one_stage, 0)
-    for m in range(2 * half):
-        orbital_copy(m, to_left).wait_send()
+    for m in range(slots):
+        device = to_left if m < half else to_right
+        for group in range(2):
+            if m % half == half - 1:
+                orbital_copy(m, group, device).wait_send()
+            code_copy(m, group, device).wait()
+        scale_copy(m, device).wait()
         kept_copy(m).wait()
-        code_copy(m, to_left).wait()
-        scale_copy(m, to_left).wait()
 
 
 def exchange(orbitals, pair_first, pair_second, pair_count):
@@ -350,16 +432,15 @@
     anywhere, smem = (pl.BlockSpec(memory_space=space) for space in (pl.ANY, pltpu.SMEM))
     dma, dmas = pltpu.SemaphoreType.DMA, lambda *shape: pltpu.SemaphoreType.DMA(shape)
     return pl.pallas_call(
-        functools.partial(pair_kernel, blocks, slots // 2),
+        functools.partial(pair_kernel, blocks, slots),
         out_shape=[
             jax.ShapeDtypeStruct((slots, rows, cells), f32),
             jax.ShapeDtypeStruct((slots, rows, cells), jnp.int16),
             jax.ShapeDtypeStruct((slots, rows, LANES), f32),
-            jax.ShapeDtypeStruct(pair_second.shape, jnp.int32),
-            jax.ShapeDtypeStruct(pair_count.shape, jnp.int32),
+            jax.ShapeDtypeStruct((1, 2 * slots + 2), jnp.int32),
         ],
         in_specs=[anywhere] * (4 + len(tables)),
-        out_specs=[anywhere, anywhere, anywhere, smem, smem],
+        out_specs=[anywhere, anywhere, anywhere, smem],
         scratch_shapes=[
             pltpu.VMEM((block, rows, cells), bf16),
             pltpu.VMEM((slots, rows, cells), bf16),
@@ -367,8 +448,7 @@
             pltpu.VMEM((slots, rows, cells), f32),
             pltpu.VMEM((slots, rows, cells), jnp.int16),
             pltpu.VMEM((slots, rows, LANES), f32),
-            pltpu.VMEM((ROWS, HALF, 2 * LANES), bf16),
-            pltpu.VMEM((ROWS, HALF, 2 * LANES), bf16),
+            pltpu.VMEM((ROWS, HALF, 6 * LANES), bf16),
             pltpu.VMEM((2, ROWS, HALF, 2 * LANES), f32),
             pltpu.VMEM((2, MINE, HALF, 2 * LANES), f32),
             pltpu.VMEM((2, MINE, HALF, 2 * LANES), f32),
@@ -383,8 +463,13 @@
             pltpu.SMEM(pair_first.shape, jnp.int32),
             pltpu.SMEM(pair_second.shape, jnp.int32),
             pltpu.SMEM(pair_count.shape, jnp.int32),
-            dma, dmas(9), dmas(2), dmas(2), dmas(slots), dmas(slots),
-            dmas(slots), dmas(slots), dmas(slots), dmas(slots), dmas(slots),
+            pltpu.SMEM(pair_second.shape, jnp.int32),
+            pltpu.SMEM(pair_count.shape, jnp.int32),
+            pltpu.SMEM(pair_second.shape, jnp.int32),
+            pltpu.SMEM(pair_count.shape, jnp.int32),
+            pltpu.SemaphoreType.REGULAR, dmas(2), dmas(2),
+            dma, dmas(9), dmas(2), dmas(2), dmas(slots, 2), dmas(slots, 2),
+            dmas(slots, 2), dmas(slots, 2), dmas(slots), dmas(slots), dmas(slots),
             dmas(2), dmas(2), dmas(2), dmas(2),
         ],
         compiler_params=pltpu.CompilerParams(
@@ -395,17 +480,20 @@
 
 
 def merge_kernel(
-    half, block, kept_in, codes_in, scales_in, first, count, second, second_count,
+    half, block, kept_in, codes_in, scales_in, info,
     out, kept, codes, scales, total, zero, staged, kept_sem, code_sem, scale_sem, out_sem,
 ):
     slots = 2 * half
+    first = [info[0, slot] for slot in range(slots)]
+    second = [info[0, slots + slot] for slot in range(slots)]
+    count, second_count = info[0, 2 * slots], info[0, 2 * slots + 1]
     pieces, width = 8, zero.shape[1] // 8
 
     def own_live(slot):
-        return slot < count[0]
+        return slot < count
 
     def back_live(slot):
-        return slot < second_count[0]
+        return slot < second_count
 
     loads = []
     for m in range(slots):
@@ -420,8 +508,8 @@
     for row in range(block):
         touched = jnp.bool_(False)
         for slot in range(slots):
-            touched |= own_live(slot) & (first[0, slot] == row)
-            touched |= back_live(slot) & (second[0, slot] == row)
+            touched |= own_live(slot) & (first[slot] == row)
+            touched |= back_live(slot) & (second[slot] == row)
 
         @pl.when(jnp.logical_not(touched))
         def _():
@@ -445,7 +533,7 @@
     def add_up(place, kind_half, lead, live, rows, extra):
         several = jnp.bool_(False)
         for later in range(lead + 1, slots):
-            several |= live(later) & (rows[0, later] == rows[0, lead])
+            several |= live(later) & (rows[later] == rows[lead])
         for flag, other in extra:
             several |= flag
 
@@ -464,7 +552,7 @@
             over_pieces(begin)
             for later in range(lead + 1, slots):
 
-                @pl.when(live(later) & (rows[0, later] == rows[0, lead]))
+                @pl.when(live(later) & (rows[later] == rows[lead]))
                 def _():
                     def more(lanes):
                         total[:, lanes] += term(kind_half(later), later, lanes)
@@ -489,7 +577,7 @@
     for slot in range(slots):
         lead = back_live(slot)
         for earlier in range(slot):
-            lead &= second[0, earlier] != second[0, slot]
+            lead &= second[earlier] != second[slot]
         leads.append(lead)
 
         @pl.when(lead)
@@ -497,34 +585,34 @@
             add_up(slot, lambda s: s >= half, slot, back_live, second, [])
             owned = jnp.bool_(False)
             for other in range(slots):
-                owned |= own_live(other) & (first[0, other] == second[0, slot])
+                owned |= own_live(other) & (first[other] == second[slot])
 
             @pl.when(jnp.logical_not(owned))
             def _():
-                pltpu.make_async_copy(staged.at[slot], out.at[second[0, slot]], out_sem).start()
+                pltpu.make_async_copy(staged.at[slot], out.at[second[slot]], out_sem).start()
 
     for slot in range(slots):
         lead = own_live(slot)
         for earlier in range(slot):
-            lead &= first[0, earlier] != first[0, slot]
+            lead &= first[earlier] != first[slot]
 
         @pl.when(lead)
         def _():
-            extra = [(leads[other] & (second[0, other] == first[0, slot]), other) for other in range(slots)]
+            extra = [(leads[other] & (second[other] == first[slot]), other) for other in range(slots)]
             add_up(slots + slot, lambda s: s < half, slot, own_live, first, extra)
-            pltpu.make_async_copy(staged.at[slots + slot], out.at[first[0, slot]], out_sem).start()
+            pltpu.make_async_copy(staged.at[slots + slot], out.at[first[slot]], out_sem).start()
 
     pltpu.make_async_copy(out, out, out_sem).wait()
 
 
-def merge(kept, codes, scales, pair_first, pair_count, next_second, next_count, shape):
+def merge(kept, codes, scales, info, shape):
     slots, rows, cells = kept.shape
     anywhere, smem = (pl.BlockSpec(memory_space=space) for space in (pl.ANY, pltpu.SMEM))
     dma, dmas = pltpu.SemaphoreType.DMA, pltpu.SemaphoreType.DMA((slots,))
     return pl.pallas_call(
         functools.partial(merge_kernel, slots // 2, shape[0]),
         out_shape=jax.ShapeDtypeStruct(shape, bf16),
-        in_specs=[anywhere] * 3 + [smem] * 4,
+        in_specs=[anywhere] * 3 + [smem],
         out_specs=anywhere,
         scratch_shapes=[
             pltpu.VMEM(kept.shape, f32),
@@ -537,12 +625,12 @@
         ],
         compiler_params=pltpu.CompilerParams(vmem_limit_bytes=60 * 2**20),
         name="merge_rows",
-    )(kept, codes, scales, pair_first, pair_count, next_second, next_count)
+    )(kept, codes, scales, info)
 
 
 def per_device(orbitals, pair_first, pair_second, pair_count):
-    kept, codes, scales, next_second, next_count = exchange(orbitals, pair_first, pair_second, pair_count)
-    return merge(kept, codes, scales, pair_first, pair_count, next_second, next_count, orbitals.shape)
+    kept, codes, scales, info = exchange(orbitals, pair_first, pair_second, pair_count)
+    return merge(kept, codes, scales, info, orbitals.shape)
 
 
 def solution(mesh):

time: 52.1 us -> 49.6 us (0.952)
  Pallas kernels: 50.8 us -> 48.3 us
    pallas_call x1, Pallas kernels: 6.43 us -> 5.08 us  [merge(): pl.pallas_call(functools.partial(merge_kernel, slots // 2, shape[0]), out...]
    pallas_call x1, Pallas kernels: 44.3 us -> 43.2 us  [exchange(): pl.pallas_call(functools.partial(pair_kernel, blocks, slots), out_shape=[...]
where the time goes in v4:
time: 49.6 us; the launch traced here: 48.9 us
  Pallas kernels  48.3 us (97%)
  between operations  0.66 us (1%)
    pallas_call x1, Pallas kernels, exchange(): pl.pallas_call(functools.partial(pair_kernel, blocks, slots), out_shape=[...  43.2 us
    pallas_call x1, Pallas kernels, merge(): pl.pallas_call(functools.partial(merge_kernel, slots // 2, shape[0]), out...  5.08 us

profile of v4, /device:TPU:0, one launch (start us, length us, event | category | flops | bytes accessed | tf_op | source)
XLA Modules:
  0.0 48.9 jit_solution(693256964992775085)
XLA Ops:
  0.7 43.2 %pair_exchange.1 = (f32[4,32,4096]{2,1,0:T(8,128)}, s16[4,32,4096]{2,1,0:T(8,128)(2,1)}, f32[4,32,128]{2,1,0:T(8,128)}, s32[1,10]{1,0:T(1,128)}) custom-call(bf16[32,32,4096]{2,1,0:T(8,128)(2,1)} %orbitals.1, s32[1,4]{1,0:T(1,128)} %first_in.1, s32[1,4]{1,0:T(1,128)} %second_in.1, s32[1]{0:T(128)S(6)} %copy.11.count_in, ...), custom_call_target="tpu_custom_call" | custom-call | tf_op jit(solution)/shard_map/pair_exchange/pallas_call | solution.py:434
  43.9 5.1 %merge_rows.1 = bf16[32,32,4096]{2,1,0:T(8,128)(2,1)} custom-call(f32[4,32,4096]{2,1,0:T(8,128)} %get-tuple-element.9.kept_in, s16[4,32,4096]{2,1,0:T(8,128)(2,1)} %get-tuple-element.10.codes_in, f32[4,32,128]{2,1,0:T(8,128)} %get-tuple-element.11.scales_in, s32[1,10]{1,0:T(1,128)} %get-tuple-element.12.info), custom_call_target="tpu_custom_call" | custom-call | tf_op jit(solution)/shard_map/merge_rows/pallas_call | solution.py:612

commit v5 on v4

--- a/solution.py
+++ b/solution.py
@@ -16,7 +16,7 @@
 HALF = L // 2
 LANES = 128
 ROWS = 17
-MINE = 9
+LOADS = 4
 CODE = 32767.0
 f32 = jnp.float32
 bf16 = jnp.bfloat16
@@ -44,15 +44,9 @@
     position = np.arange(L)
     angle = 2.0 * np.pi * (np.outer(position, position) % L) / L
     both = np.concatenate([np.cos(angle), np.sin(angle)], 0)
-    forwards, inverses = [], []
-    for core in range(2):
-        order = np.concatenate([np.arange(HALF) + HALF * core, np.arange(HALF) + HALF * (1 - core)])
-        high, low = split_table(both[:, order])
-        forwards.append(np.concatenate([high, high, low], 1))
-        back = np.concatenate([both[:L, order].T, both[L:, order].T], 0)
-        high, low = split_table(back)
-        inverses.append(np.concatenate([high, high, low], 1))
-    return np.stack(forwards), np.stack(inverses)
+    high, low = split_table(both)
+    table = np.concatenate([high, high, low], 1)
+    return table, table
 
 
 def filter_table():
@@ -130,43 +124,49 @@
     orbitals, first_in, second_in, count_in,
     lane_fwd, lane_inv, row_fwd, row_inv, filters, twiddles,
     kept_out, codes_out, scales_out, info,
-    orb, sending, arriving, kept, codes, scales,
-    spectra, planes, others, filtered, returned, result,
+    orb, sending, arriving, sharing, whole, kept, codes, scales,
+    spectra, planes, result,
     lane_fwd_v, lane_inv_v, row_fwd_v, row_inv_v, filters_v, twiddles_v, first_s, second_s, count_s,
-    next_second, next_count, relay_second, relay_count, final_here, relay_send, relay_recv, load_sem, table_sem, index_send, index_recv, orbital_send, orbital_recv,
-    code_send, code_recv, scale_send, scale_recv, kept_sem,
-    first_send, first_recv, second_send, second_recv,
+    next_second, next_count, relay_second, relay_count, final_here, relay_send, relay_recv, load_sem,
+    table_sem, index_send, index_recv, orbital_send, orbital_recv,
+    share_send, share_recv, code_send, code_recv, scale_send, scale_recv, kept_sem, kept_send, kept_recv,
 ):
     half = slots // 2
     me, core = lax.axis_index("blk"), lax.axis_index("grid")
     right, left = lax.rem(me + 1, blocks), lax.rem(me + blocks - 1, blocks)
-    to_right, to_left, to_partner = {"blk": right}, {"blk": left}, {"grid": 1 - core}
+    to_partner = {"grid": 1 - core}
 
     final, relay = blocks - 1, max(2, blocks // 4) - 1
-    is_first, is_final, is_relay = me == 0, me == final, me == relay
+    is_first, is_final = me == 0, me == final
+    sends_index, is_relay = core == 1, (me == relay) & (core == 1)
     barrier = pltpu.get_barrier_semaphore()
-    for device in (to_left, to_partner):
-        pl.semaphore_signal(barrier, inc=1, device_id=device)
+    for place in range(2):
+        pl.semaphore_signal(barrier, inc=1, device_id={"blk": left, "grid": place})
+    pl.semaphore_signal(barrier, inc=1, device_id=to_partner)
 
     @pl.when(jnp.logical_not(is_final))
     def _():
-        pl.semaphore_signal(barrier, inc=1, device_id=to_right)
+        for place in range(2):
+            pl.semaphore_signal(barrier, inc=1, device_id={"blk": right, "grid": place})
 
     @pl.when(is_relay)
     def _():
-        pl.semaphore_signal(barrier, inc=1, device_id={"blk": 0})
-        pl.semaphore_signal(barrier, inc=1, device_id={"blk": final})
-
-    load = pltpu.make_async_copy(orbitals, orb, load_sem)
-    load.start()
-    base = 8 * core
+        for device in ({"blk": 0, "grid": 1}, {"blk": final, "grid": 0}, {"blk": final, "grid": 1}):
+            pl.semaphore_signal(barrier, inc=1, device_id=device)
+
+    size = orb.shape[0] // LOADS
+    loads = [
+        pltpu.make_async_copy(orbitals.at[pl.ds(size * n, size)], orb.at[pl.ds(size * n, size)], load_sem.at[n])
+        for n in range(LOADS)
+    ]
+    for load in loads:
+        load.start()
     tables = [
         pltpu.make_async_copy(source, target, table_sem.at[place])
         for place, (source, target) in enumerate([
             (first_in, first_s), (second_in, second_s), (count_in, count_s),
-            (lane_fwd, lane_fwd_v), (lane_inv, lane_inv_v),
-            (row_fwd.at[core], row_fwd_v), (row_inv.at[core], row_inv_v),
-            (filters.at[pl.ds(base, MINE)], filters_v), (twiddles, twiddles_v),
+            (lane_fwd, lane_fwd_v), (lane_inv, lane_inv_v), (row_fwd, row_fwd_v), (row_inv, row_inv_v),
+            (filters, filters_v), (twiddles, twiddles_v),
         ])
     ]
     for table in tables:
@@ -183,121 +183,171 @@
             for part, (source, target) in enumerate(zip(sources, targets))
         ]
 
-    to_next = index_copies((next_second, next_count), index_send, index_recv, to_left)
-    to_relay = index_copies((relay_second, relay_count), index_send, relay_recv, {"blk": relay})
-
-    def orbital_copy(m, group, device):
-        part = pl.ds(16 * group, 16)
+    def to_both(block, sent, sources=(second_in, count_in)):
+        targets = (next_second, next_count)
+        return [
+            copy
+            for place in range(2)
+            for copy in index_copies(targets, sent.at[place], index_recv, {"blk": block, "grid": place}, sources)
+        ]
+
+    to_next = to_both(left, index_send)
+    to_relay = index_copies((relay_second, relay_count), index_send.at[0], relay_recv, {"blk": relay, "grid": 1})
+
+    def orbital_copy(m, group):
+        visits = m < half
+        device = {"blk": right if visits else left, "grid": 1 if visits else 0}
+        place = 2 * core + group
         return remote(
-            sending.at[m, part], arriving.at[m, part], orbital_send.at[m, group], orbital_recv.at[m, group], device
+            sending.at[m, pl.ds(16 * group, 16)],
+            arriving.at[m % half, pl.ds(pl.multiple_of(16 * place, 16), 16)],
+            orbital_send.at[m, group], orbital_recv.at[m % half, place], device,
         )
 
-    def send_first(m, device):
+    def arrival(stage, place):
+        rows = pl.ds(pl.multiple_of(16 * place, 16), 16)
+        return remote(
+            sending.at[0, pl.ds(0, 16)], arriving.at[stage, rows],
+            orbital_send.at[0, 0], orbital_recv.at[stage, place], to_partner,
+        )
+
+    def worked_on(stage, by):
+        return jnp.where(by == 1, first_s[0, stage], next_second[0, half + stage])
+
+    def share_copy(stage):
+        rows = pl.ds(pl.multiple_of(HALF * core, HALF), HALF)
+        return remote(sharing.at[stage], whole.at[stage, rows], share_send.at[stage], share_recv.at[stage], to_partner)
+
+    def send_first(m):
         for group in range(2):
-            orbital_copy(m, group, device).start()
+            orbital_copy(m, group).start()
 
     def load_own():
         for table in tables[:3]:
             table.wait()
-        load.wait()
+        for load in loads:
+            load.wait()
         for m in range(half, slots):
             sending[m] = orb[first_s[0, m]]
 
     def load_visits():
-        for copy in to_next:
+        for copy in to_next[:2]:
             copy.wait_recv()
         for m in range(half):
             sending[m] = orb[next_second[0, m]]
 
-    @pl.when(jnp.logical_not(is_final))
-    def _():
-        pl.semaphore_wait(barrier, 3)
+    normal = 5 + is_final.astype(jnp.int32)
+    pl.semaphore_wait(barrier, jnp.where(is_first, 3 + core, normal))
 
     @pl.when(is_final)
     def _():
-        pl.semaphore_wait(barrier, 4)
-        pl.semaphore_signal(final_here, inc=1, device_id=to_right)
-        pl.semaphore_signal(final_here, inc=1, device_id={"blk": relay})
+        for place in range(2):
+            pl.semaphore_signal(final_here, inc=1, device_id={"blk": right, "grid": place})
+        pl.semaphore_signal(final_here, inc=1, device_id={"blk": relay, "grid": 1})
 
     @pl.when(is_first)
     def _():
-        for copy in to_relay:
-            copy.start()
+        @pl.when(sends_index)
+        def _():
+            for copy in to_relay:
+                copy.start()
+
         load_own()
         load_visits()
-        send_first(0, to_right)
-        pl.semaphore_wait(final_here, 1)
-        send_first(half, to_left)
+        send_first(0)
+        pl.semaphore_wait(final_here, 2)
+        send_first(half)
+
+        @pl.when(sends_index)
+        def _():
+            for copy in to_relay:
+                copy.wait_send()
 
     @pl.when(jnp.logical_not(is_first))
     def _():
-        for copy in to_next:
-            copy.start()
+        @pl.when(sends_index)
+        def _():
+            for copy in to_next:
+                copy.start()
+
         load_own()
-        send_first(half, to_left)
+        send_first(half)
 
         @pl.when(is_relay)
         def _():
             for copy in to_relay:
                 copy.wait_recv()
-            pl.semaphore_wait(final_here, 1)
-            onward = index_copies(
-                (next_second, next_count), relay_send, index_recv, {"blk": final}, (relay_second, relay_count)
-            )
+            pl.semaphore_wait(final_here, 2)
+            onward = to_both(final, relay_send, (relay_second, relay_count))
             for copy in onward:
                 copy.start()
             for copy in onward:
                 copy.wait_send()
 
         load_visits()
-        send_first(0, to_right)
-
-    for copy in to_next:
-        copy.wait_send()
+        send_first(0)
+
+        @pl.when(sends_index)
+        def _():
+            for copy in to_next:
+                copy.wait_send()
+
+    for stage in range(half):
+        sharing[stage] = orb[worked_on(stage, 1 - core)]
+        share_copy(stage).start()
+        whole[stage, pl.ds(pl.multiple_of(HALF * core, HALF), HALF)] = orb[worked_on(stage, core)]
     for stage in range(1, half):
         for group in range(2):
-            for m, device in ((half + stage, to_left), (stage, to_right)):
-                orbital_copy(m - 1, group, device).wait_send()
-                orbital_copy(m, group, device).start()
+            for m in (half + stage, stage):
+                orbital_copy(m - 1, group).wait_send()
+                orbital_copy(m, group).start()
     for table in tables[3:]:
         table.wait()
-
-    def kept_copy(m):
-        return pltpu.make_async_copy(kept.at[m], kept_out.at[m], kept_sem.at[m])
-
-    def code_copy(m, group, device):
-        part = pl.ds(16 * group, 16)
+    for m in range(slots):
+        info[0, m] = first_s[0, m]
+        info[0, slots + m] = next_second[0, m]
+    info[0, 2 * slots] = count_s[0]
+    info[0, 2 * slots + 1] = next_count[0]
+
+    def solved(stage):
+        return stage + half * (1 - core)
+
+    def kept_local(stage):
+        rows = pl.ds(pl.multiple_of(HALF * core, HALF), HALF)
+        return pltpu.make_async_copy(kept.at[stage, rows], kept_out.at[solved(stage)], kept_sem.at[stage])
+
+    def kept_remote(stage, m):
+        rows = pl.ds(pl.multiple_of(HALF * (1 - core), HALF), HALF)
+        return remote(kept.at[stage, rows], kept_out.at[m], kept_send.at[stage], kept_recv.at[stage], to_partner)
+
+    def code_copy(stage, place, m):
+        device = {"blk": jnp.where(core == 1, left, right), "grid": lax.div(place, 2)}
+        rows = pl.ds(pl.multiple_of(16 * place, 16), 16)
+        there = pl.ds(pl.multiple_of(16 * lax.rem(place, 2), 16), 16)
         return remote(
-            codes.at[m, part], codes_out.at[m, part], code_send.at[m, group], code_recv.at[m, group], device
+            codes.at[stage, rows], codes_out.at[m, there],
+            code_send.at[stage, place], code_recv.at[m, lax.rem(place, 2)], device,
         )
 
-    def scale_copy(m, device):
-        return remote(scales.at[m], scales_out.at[m], scale_send.at[m], scale_recv.at[m], device)
-
-    other_base = 8 * (1 - core)
-
-    def first_copy(which):
+    def scale_copy(stage, place, m):
+        device = {"blk": jnp.where(core == 1, left, right), "grid": place}
         return remote(
-            planes.at[which, pl.ds(other_base, MINE)], others.at[which],
-            first_send.at[which], first_recv.at[which], to_partner,
+            scales.at[stage, pl.ds(HALF * place, HALF)], scales_out.at[m],
+            scale_send.at[stage, place], scale_recv.at[m], device,
         )
 
-    def second_copy(which):
-        return remote(
-            filtered.at[which, pl.ds(core, 8)], returned.at[which, pl.ds(base + core, 8)],
-            second_send.at[which], second_recv.at[which], to_partner,
-        )
-
-    def forward(stage, which):
-        m, here = stage + half * which, jnp.where(which == 0, first_s[0, stage], next_second[0, half + stage])
-
-        def forward_group(group, carry):
-            orbital_copy(m, group, to_left).wait_recv()
-            rows = pl.ds(pl.multiple_of(16 * group, 16), 16)
+    def one_stage(stage, carry):
+        m = solved(stage)
+        share_copy(stage).wait_recv()
+
+        def forward_group(turn, carry):
+            place = 2 * lax.rem(turn, 2) + lax.div(turn, 2)
+            rows = pl.ds(pl.multiple_of(16 * place, 16), 16)
+            arrival(stage, place).wait_recv()
             values = []
             for column in range(HALF):
                 lanes = pl.ds(LANES * column, LANES)
-                values.append(orb[here, rows, lanes].astype(f32) * arriving[m, rows, lanes].astype(f32))
+                values.append(whole[stage, rows, lanes].astype(f32) * arriving[stage, rows, lanes].astype(f32))
             re, im = real_forward(values)
             for k in range(ROWS):
                 if k == 0:
@@ -312,25 +362,15 @@
                     high, low = split(value)
                     for place, piece in enumerate((high, low, high)):
                         start = LANES * (2 * place + part)
-                        spectra[k, rows, start : start + LANES] = piece
+                        spectra[k, :, start : start + LANES] = piece
+            out = dot(spectra[...].reshape(ROWS * 16, 6 * LANES), lane_fwd_v[...])
+            planes[:, rows, :] = out.reshape(ROWS, 16, 2 * LANES)
             return carry
 
-        lax.fori_loop(0, 2, forward_group, 0)
-
-        def to_planes(start, count):
-            where = pl.ds(start, count)
-            out = dot(spectra[where].reshape(count * HALF, 6 * LANES), lane_fwd_v[...])
-            planes[which, where] = out.reshape(count, HALF, 2 * LANES)
-
-        to_planes(other_base, MINE)
-        first_copy(which).start()
-        to_planes(base + core, 8)
-
-    def solve(stage, which):
-        first_copy(which).wait()
-        for k in range(MINE):
-            values = jnp.concatenate([planes[which, base + k], others[which, k]], 0)
-            high, low = split(values)
+        lax.fori_loop(0, 4, forward_group, 0)
+
+        for k in range(ROWS):
+            high, low = split(planes[k])
             out = dot(row_fwd_v[...], jnp.concatenate([high, low, high], 0))
             kernel = filters_v[k]
             re = (out[:L, :LANES] + out[L:, LANES:]) * kernel
@@ -339,37 +379,23 @@
             out = dot(row_inv_v[...], jnp.concatenate([high, low, high], 0))
             re = out[:L, :LANES] - out[L:, LANES:]
             im = out[:L, LANES:] + out[L:, :LANES]
-            whole = jnp.concatenate([re, im], 1)
-            returned[which, base + k] = whole[:HALF]
-            filtered[which, k] = whole[HALF:]
-        second_copy(which).start()
-
-    def inverse(stage, which):
-        m, here = stage + half * which, jnp.where(which == 0, first_s[0, stage], next_second[0, half + stage])
-        live = jnp.where(m < jnp.where(which == 0, count_s[0], next_count[0]), 1.0, 0.0).astype(f32)
-        device = {"blk": jnp.where(which == 0, left, right)}
-
-        def from_planes(start, count):
-            where = pl.ds(start, count)
-            values = returned[which, where].reshape(count * HALF, 2 * LANES)
-            high, low = split(values)
+            planes[k] = jnp.concatenate([re, im], 1)
+
+        live = jnp.where(m < jnp.where(core == 1, count_s[0], next_count[0]), 1.0, 0.0).astype(f32)
+
+        def inverse_group(place, carry):
+            rows = pl.ds(pl.multiple_of(16 * place, 16), 16)
+            high, low = split(planes[:, rows, :].reshape(ROWS * 16, 2 * LANES))
             out = dot(jnp.concatenate([high, low, high], 1), lane_inv_v[...])
-            result[where] = out.reshape(count, HALF, 2 * LANES)
-
-        from_planes(base, MINE)
-        second_copy(which).wait()
-        from_planes(9 * (1 - core), 8)
-
-        def inverse_group(group, carry):
-            rows = pl.ds(pl.multiple_of(16 * group, 16), 16)
+            result[...] = out.reshape(ROWS, 16, 2 * LANES)
             re, im = [], []
             for k in range(ROWS):
-                value_re = result[k, rows, :LANES]
+                value_re = result[k, :, :LANES]
                 if k == 0:
                     re.append(value_re)
                     im.append(None)
                     continue
-                value_im = result[k, rows, LANES:]
+                value_im = result[k, :, LANES:]
                 c, s = twiddles_v[k, 0:1], twiddles_v[k, 1:2]
                 re.append(value_re * c + value_im * s)
                 im.append(None if k == ROWS - 1 else value_im * c - value_re * s)
@@ -378,48 +404,42 @@
             for column in range(HALF):
                 lanes = pl.ds(LANES * column, LANES)
                 value = potential[column] * live
-                kept[m, rows, lanes] = value * arriving[m, rows, lanes].astype(f32)
-                terms.append(value * orb[here, rows, lanes].astype(f32))
+                kept[stage, rows, lanes] = value * arriving[stage, rows, lanes].astype(f32)
+                terms.append(value * whole[stage, rows, lanes].astype(f32))
                 size = jnp.abs(terms[-1])
                 largest = size if largest is None else jnp.maximum(largest, size)
             bound = jnp.maximum(jnp.max(largest, axis=1, keepdims=True), 1e-30)
-            scales[m, rows, :] = jnp.broadcast_to(bound * (1.0 / CODE), (16, LANES))
+            scales[stage, rows, :] = jnp.broadcast_to(bound * (1.0 / CODE), (16, LANES))
             inverse_scale = CODE / bound
             for column in range(HALF):
                 lanes = pl.ds(LANES * column, LANES)
                 code = jnp.round(terms[column] * inverse_scale)
-                codes[m, rows, lanes] = code.astype(jnp.int32).astype(jnp.int16)
-            code_copy(m, group, device).start()
+                codes[stage, rows, lanes] = code.astype(jnp.int32).astype(jnp.int16)
+            code_copy(stage, place, m).start()
             return carry
 
-        lax.fori_loop(0, 2, inverse_group, 0)
-        scale_copy(m, device).start()
-        kept_copy(m).start()
-
-    def one_stage(stage, carry):
-        for phase in (forward, solve, inverse):
-            def one_slot(turn, carry):
-                phase(stage, 1 - turn)
-                return carry
-
-            lax.fori_loop(0, 2, one_slot, 0)
+        lax.fori_loop(0, 4, inverse_group, 0)
+        for place in range(2):
+            scale_copy(stage, place, m).start()
+        kept_local(stage).start()
+        kept_remote(stage, m).start()
         return carry
 
+    lax.fori_loop(0, half, one_stage, 0)
+    for stage in range(half):
+        share_copy(stage).wait_send()
+        kept_local(stage).wait()
+        kept_remote(stage, stage + half * core).wait()
+        for place in range(4):
+            code_copy(stage, place, solved(stage)).wait_send()
+        for place in range(2):
+            scale_copy(stage, place, solved(stage)).wait_send()
     for m in range(slots):
-        info[0, m] = first_s[0, m]
-        info[0, slots + m] = next_second[0, m]
-    info[0, 2 * slots] = count_s[0]
-    info[0, 2 * slots + 1] = next_count[0]
-
-    lax.fori_loop(0, half, one_stage, 0)
-    for m in range(slots):
-        device = to_left if m < half else to_right
         for group in range(2):
             if m % half == half - 1:
-                orbital_copy(m, group, device).wait_send()
-            code_copy(m, group, device).wait()
-        scale_copy(m, device).wait()
-        kept_copy(m).wait()
+                orbital_copy(m, group).wait_send()
+            code_copy(0, group, m).wait_recv()
+        scale_copy(0, 0, m).wait_recv()
 
 
 def exchange(orbitals, pair_first, pair_second, pair_count):
@@ -431,6 +451,7 @@
     tables = [jnp.asarray(t) for t in (lane_fwd, lane_inv, row_fwd, row_inv, filter_table(), twiddle_table())]
     anywhere, smem = (pl.BlockSpec(memory_space=space) for space in (pl.ANY, pltpu.SMEM))
     dma, dmas = pltpu.SemaphoreType.DMA, lambda *shape: pltpu.SemaphoreType.DMA(shape)
+    half = slots // 2
     return pl.pallas_call(
         functools.partial(pair_kernel, blocks, slots),
         out_shape=[
@@ -444,21 +465,20 @@
         scratch_shapes=[
             pltpu.VMEM((block, rows, cells), bf16),
             pltpu.VMEM((slots, rows, cells), bf16),
-            pltpu.VMEM((slots, rows, cells), bf16),
-            pltpu.VMEM((slots, rows, cells), f32),
-            pltpu.VMEM((slots, rows, cells), jnp.int16),
-            pltpu.VMEM((slots, rows, LANES), f32),
-            pltpu.VMEM((ROWS, HALF, 6 * LANES), bf16),
-            pltpu.VMEM((2, ROWS, HALF, 2 * LANES), f32),
-            pltpu.VMEM((2, MINE, HALF, 2 * LANES), f32),
-            pltpu.VMEM((2, MINE, HALF, 2 * LANES), f32),
-            pltpu.VMEM((2, ROWS, HALF, 2 * LANES), f32),
-            pltpu.VMEM((ROWS, HALF, 2 * LANES), f32),
+            pltpu.VMEM((half, L, cells), bf16),
+            pltpu.VMEM((half, rows, cells), bf16),
+            pltpu.VMEM((half, L, cells), bf16),
+            pltpu.VMEM((half, L, cells), f32),
+            pltpu.VMEM((half, L, cells), jnp.int16),
+            pltpu.VMEM((half, L, LANES), f32),
+            pltpu.VMEM((ROWS, 16, 6 * LANES), bf16),
+            pltpu.VMEM((ROWS, L, 2 * LANES), f32),
+            pltpu.VMEM((ROWS, 16, 2 * LANES), f32),
             pltpu.VMEM(lane_fwd.shape, bf16),
             pltpu.VMEM(lane_inv.shape, bf16),
-            pltpu.VMEM(row_fwd.shape[1:], bf16),
-            pltpu.VMEM(row_inv.shape[1:], bf16),
-            pltpu.VMEM((MINE, L, LANES), f32),
+            pltpu.VMEM(row_fwd.shape, bf16),
+            pltpu.VMEM(row_inv.shape, bf16),
+            pltpu.VMEM((ROWS, L, LANES), f32),
             pltpu.VMEM((ROWS, 2, LANES), f32),
             pltpu.SMEM(pair_first.shape, jnp.int32),
             pltpu.SMEM(pair_second.shape, jnp.int32),
@@ -467,10 +487,10 @@
             pltpu.SMEM(pair_count.shape, jnp.int32),
             pltpu.SMEM(pair_second.shape, jnp.int32),
             pltpu.SMEM(pair_count.shape, jnp.int32),
-            pltpu.SemaphoreType.REGULAR, dmas(2), dmas(2),
-            dma, dmas(9), dmas(2), dmas(2), dmas(slots, 2), dmas(slots, 2),
-            dmas(slots, 2), dmas(slots, 2), dmas(slots), dmas(slots), dmas(slots),
-            dmas(2), dmas(2), dmas(2), dmas(2),
+            pltpu.SemaphoreType.REGULAR, dmas(2, 2), dmas(2), dmas(LOADS),
+            dmas(9), dmas(2, 2), dmas(2), dmas(slots, 2), dmas(half, 4),
+            dmas(half), dmas(half), dmas(half, 4), dmas(slots, 2), dmas(half, 2), dmas(slots),
+            dmas(half), dmas(half), dmas(half),
         ],
         compiler_params=pltpu.CompilerParams(
             collective_id=0, has_side_effects=True, vmem_limit_bytes=60 * 2**20

time: 49.6 us -> 48.5 us (0.978)
  the two profiles are of different devices: /device:TPU:0 before, /device:TPU:1 now
where the time goes in v5:
time: 48.5 us; the launch traced here: 48.3 us
  Pallas kernels  47.7 us (98%)
  between operations  0.66 us (1%)
    pallas_call x1, Pallas kernels, exchange(): pl.pallas_call(functools.partial(pair_kernel, blocks, slots), out_shape=[...  41.9 us
    pallas_call x1, Pallas kernels, merge(): pl.pallas_call(functools.partial(merge_kernel, slots // 2, shape[0]), out...  5.73 us

profile of v5, /device:TPU:1, one launch (start us, length us, event | category | flops | bytes accessed | tf_op | source)
XLA Modules:
  0.0 48.3 jit_solution(13862296724015313727)
XLA Ops:
  0.7 41.9 %pair_exchange.1 = (f32[4,32,4096]{2,1,0:T(8,128)}, s16[4,32,4096]{2,1,0:T(8,128)(2,1)}, f32[4,32,128]{2,1,0:T(8,128)}, s32[1,10]{1,0:T(1,128)}) custom-call(bf16[32,32,4096]{2,1,0:T(8,128)(2,1)} %orbitals.1, s32[1,4]{1,0:T(1,128)} %first_in.1, s32[1,4]{1,0:T(1,128)} %second_in.1, s32[1]{0:T(128)S(6)} %copy.10.count_in, ...), custom_call_target="tpu_custom_call" | custom-call | tf_op jit(solution)/shard_map/pair_exchange/pallas_call | solution.py:455
  42.6 5.7 %merge_rows.1 = bf16[32,32,4096]{2,1,0:T(8,128)(2,1)} custom-call(f32[4,32,4096]{2,1,0:T(8,128)} %get-tuple-element.9.kept_in, s16[4,32,4096]{2,1,0:T(8,128)(2,1)} %get-tuple-element.10.codes_in, f32[4,32,128]{2,1,0:T(8,128)} %get-tuple-element.11.scales_in, s32[1,10]{1,0:T(1,128)} %get-tuple-element.12.info), custom_call_target="tpu_custom_call" | custom-call | tf_op jit(solution)/shard_map/merge_rows/pallas_call | solution.py:632

commit v6 on v5

--- a/solution.py
+++ b/solution.py
@@ -18,6 +18,8 @@
 ROWS = 17
 LOADS = 4
 CODE = 32767.0
+MANTISSA = 16384.0
+CELLS = L * L
 f32 = jnp.float32
 bf16 = jnp.bfloat16
 
@@ -115,6 +117,10 @@
     return high, (values - high.astype(f32)).astype(bf16)
 
 
+def scale_of(mantissa, exponent):
+    return mantissa * jnp.exp2(exponent) * (1.0 / (MANTISSA * CODE))
+
+
 def dot(left, right):
     return jnp.dot(left, right, preferred_element_type=f32)
 
@@ -123,13 +129,13 @@
     blocks, slots,
     orbitals, first_in, second_in, count_in,
     lane_fwd, lane_inv, row_fwd, row_inv, filters, twiddles,
-    kept_out, codes_out, scales_out, info,
-    orb, sending, arriving, sharing, whole, kept, codes, scales,
+    kept_out, codes_out, info,
+    orb, sending, arriving, sharing, whole, kept, codes,
     spectra, planes, result,
     lane_fwd_v, lane_inv_v, row_fwd_v, row_inv_v, filters_v, twiddles_v, first_s, second_s, count_s,
     next_second, next_count, relay_second, relay_count, final_here, relay_send, relay_recv, load_sem,
     table_sem, index_send, index_recv, orbital_send, orbital_recv,
-    share_send, share_recv, code_send, code_recv, scale_send, scale_recv, kept_sem, kept_send, kept_recv,
+    share_send, share_recv, code_send, code_recv, kept_sem, kept_send, kept_recv,
 ):
     half = slots // 2
     me, core = lax.axis_index("blk"), lax.axis_index("grid")
@@ -196,7 +202,7 @@
 
     def orbital_copy(m, group):
         visits = m < half
-        device = {"blk": right if visits else left, "grid": 1 if visits else 0}
+        device = {"blk": right if visits else left, "grid": 0 if visits else 1}
         place = 2 * core + group
         return remote(
             sending.at[m, pl.ds(16 * group, 16)],
@@ -212,7 +218,7 @@
         )
 
     def worked_on(stage, by):
-        return jnp.where(by == 1, first_s[0, stage], next_second[0, half + stage])
+        return jnp.where(by == 0, first_s[0, stage], next_second[0, half + stage])
 
     def share_copy(stage):
         rows = pl.ds(pl.multiple_of(HALF * core, HALF), HALF)
@@ -310,7 +316,7 @@
     info[0, 2 * slots + 1] = next_count[0]
 
     def solved(stage):
-        return stage + half * (1 - core)
+        return stage + half * core
 
     def kept_local(stage):
         rows = pl.ds(pl.multiple_of(HALF * core, HALF), HALF)
@@ -321,19 +327,12 @@
         return remote(kept.at[stage, rows], kept_out.at[m], kept_send.at[stage], kept_recv.at[stage], to_partner)
 
     def code_copy(stage, place, m):
-        device = {"blk": jnp.where(core == 1, left, right), "grid": lax.div(place, 2)}
+        device = {"blk": jnp.where(core == 0, left, right), "grid": lax.div(place, 2)}
         rows = pl.ds(pl.multiple_of(16 * place, 16), 16)
         there = pl.ds(pl.multiple_of(16 * lax.rem(place, 2), 16), 16)
         return remote(
             codes.at[stage, rows], codes_out.at[m, there],
             code_send.at[stage, place], code_recv.at[m, lax.rem(place, 2)], device,
-        )
-
-    def scale_copy(stage, place, m):
-        device = {"blk": jnp.where(core == 1, left, right), "grid": place}
-        return remote(
-            scales.at[stage, pl.ds(HALF * place, HALF)], scales_out.at[m],
-            scale_send.at[stage, place], scale_recv.at[m], device,
         )
 
     def one_stage(stage, carry):
@@ -381,7 +380,7 @@
             im = out[:L, LANES:] + out[L:, :LANES]
             planes[k] = jnp.concatenate([re, im], 1)
 
-        live = jnp.where(m < jnp.where(core == 1, count_s[0], next_count[0]), 1.0, 0.0).astype(f32)
+        live = jnp.where(m < jnp.where(core == 0, count_s[0], next_count[0]), 1.0, 0.0).astype(f32)
 
         def inverse_group(place, carry):
             rows = pl.ds(pl.multiple_of(16 * place, 16), 16)
@@ -408,9 +407,12 @@
                 terms.append(value * whole[stage, rows, lanes].astype(f32))
                 size = jnp.abs(terms[-1])
                 largest = size if largest is None else jnp.maximum(largest, size)
-            bound = jnp.maximum(jnp.max(largest, axis=1, keepdims=True), 1e-30)
-            scales[stage, rows, :] = jnp.broadcast_to(bound * (1.0 / CODE), (16, LANES))
-            inverse_scale = CODE / bound
+            bound = jnp.broadcast_to(jnp.maximum(jnp.max(largest, axis=1, keepdims=True), 1e-30), (16, LANES))
+            exponent = jnp.ceil(jnp.log2(bound))
+            mantissa = jnp.ceil(bound * jnp.exp2(-exponent) * MANTISSA)
+            side = lax.broadcasted_iota(jnp.int32, (16, LANES), 1) < LANES // 2
+            codes[stage, rows, CELLS:] = jnp.where(side, mantissa, exponent).astype(jnp.int32).astype(jnp.int16)
+            inverse_scale = 1.0 / scale_of(mantissa, exponent)
             for column in range(HALF):
                 lanes = pl.ds(LANES * column, LANES)
                 code = jnp.round(terms[column] * inverse_scale)
@@ -419,8 +421,6 @@
             return carry
 
         lax.fori_loop(0, 4, inverse_group, 0)
-        for place in range(2):
-            scale_copy(stage, place, m).start()
         kept_local(stage).start()
         kept_remote(stage, m).start()
         return carry
@@ -429,17 +429,14 @@
     for stage in range(half):
         share_copy(stage).wait_send()
         kept_local(stage).wait()
-        kept_remote(stage, stage + half * core).wait()
+        kept_remote(stage, stage + half * (1 - core)).wait()
         for place in range(4):
             code_copy(stage, place, solved(stage)).wait_send()
-        for place in range(2):
-            scale_copy(stage, place, solved(stage)).wait_send()
     for m in range(slots):
         for group in range(2):
             if m % half == half - 1:
                 orbital_copy(m, group).wait_send()
             code_copy(0, group, m).wait_recv()
-        scale_copy(0, 0, m).wait_recv()
 
 
 def exchange(orbitals, pair_first, pair_second, pair_count):
@@ -456,12 +453,11 @@
         functools.partial(pair_kernel, blocks, slots),
         out_shape=[
             jax.ShapeDtypeStruct((slots, rows, cells), f32),
-            jax.ShapeDtypeStruct((slots, rows, cells), jnp.int16),
-            jax.ShapeDtypeStruct((slots, rows, LANES), f32),
+            jax.ShapeDtypeStruct((slots, rows, cells + LANES), jnp.int16),
             jax.ShapeDtypeStruct((1, 2 * slots + 2), jnp.int32),
         ],
         in_specs=[anywhere] * (4 + len(tables)),
-        out_specs=[anywhere, anywhere, anywhere, smem],
+        out_specs=[anywhere, anywhere, smem],
         scratch_shapes=[
             pltpu.VMEM((block, rows, cells), bf16),
             pltpu.VMEM((slots, rows, cells), bf16),
@@ -469,8 +465,7 @@
             pltpu.VMEM((half, rows, cells), bf16),
             pltpu.VMEM((half, L, cells), bf16),
             pltpu.VMEM((half, L, cells), f32),
-            pltpu.VMEM((half, L, cells), jnp.int16),
-            pltpu.VMEM((half, L, LANES), f32),
+            pltpu.VMEM((half, L, cells + LANES), jnp.int16),
             pltpu.VMEM((ROWS, 16, 6 * LANES), bf16),
             pltpu.VMEM((ROWS, L, 2 * LANES), f32),
             pltpu.VMEM((ROWS, 16, 2 * LANES), f32),
@@ -489,7 +484,7 @@
             pltpu.SMEM(pair_count.shape, jnp.int32),
             pltpu.SemaphoreType.REGULAR, dmas(2, 2), dmas(2), dmas(LOADS),
             dmas(9), dmas(2, 2), dmas(2), dmas(slots, 2), dmas(half, 4),
-            dmas(half), dmas(half), dmas(half, 4), dmas(slots, 2), dmas(half, 2), dmas(slots),
+            dmas(half), dmas(half), dmas(half, 4), dmas(slots, 2),
             dmas(half), dmas(half), dmas(half),
         ],
         compiler_params=pltpu.CompilerParams(
@@ -500,14 +495,14 @@
 
 
 def merge_kernel(
-    half, block, kept_in, codes_in, scales_in, info,
-    out, kept, codes, scales, total, zero, staged, kept_sem, code_sem, scale_sem, out_sem,
+    half, block, kept_in, codes_in, info,
+    out, kept, codes, scales, total, zero, staged, kept_sem, code_sem, out_sem,
 ):
     slots = 2 * half
     first = [info[0, slot] for slot in range(slots)]
     second = [info[0, slots + slot] for slot in range(slots)]
     count, second_count = info[0, 2 * slots], info[0, 2 * slots + 1]
-    pieces, width = 8, zero.shape[1] // 8
+    pieces, width = 4, zero.shape[1] // 4
 
     def own_live(slot):
         return slot < count
@@ -520,7 +515,6 @@
         kept_live, code_live = (own_live(m), back_live(m)) if m < half else (back_live(m), own_live(m))
         loads.append((kept_live, pltpu.make_async_copy(kept_in.at[m], kept.at[m], kept_sem.at[m])))
         loads.append((code_live, pltpu.make_async_copy(codes_in.at[m], codes.at[m], code_sem.at[m])))
-        loads.append((code_live, pltpu.make_async_copy(scales_in.at[m], scales.at[m], scale_sem.at[m])))
     for needed, load in loads:
         pl.when(needed)(load.start)
     zero[...] = jnp.zeros_like(zero)
@@ -537,6 +531,12 @@
 
     for needed, load in loads:
         pl.when(needed)(load.wait)
+    for m in range(slots):
+        @pl.when(back_live(m) if m < half else own_live(m))
+        def _():
+            side = codes[m, :, CELLS:].astype(f32)
+            scale = scale_of(side[:, :1], side[:, LANES // 2 : LANES // 2 + 1])
+            scales[m] = jnp.broadcast_to(scale, scales.shape[1:])
 
     def over_pieces(body):
         def piece(index, carry):
@@ -625,32 +625,32 @@
     pltpu.make_async_copy(out, out, out_sem).wait()
 
 
-def merge(kept, codes, scales, info, shape):
+def merge(kept, codes, info, shape):
     slots, rows, cells = kept.shape
     anywhere, smem = (pl.BlockSpec(memory_space=space) for space in (pl.ANY, pltpu.SMEM))
     dma, dmas = pltpu.SemaphoreType.DMA, pltpu.SemaphoreType.DMA((slots,))
     return pl.pallas_call(
         functools.partial(merge_kernel, slots // 2, shape[0]),
         out_shape=jax.ShapeDtypeStruct(shape, bf16),
-        in_specs=[anywhere] * 3 + [smem],
+        in_specs=[anywhere] * 2 + [smem],
         out_specs=anywhere,
         scratch_shapes=[
             pltpu.VMEM(kept.shape, f32),
             pltpu.VMEM(codes.shape, jnp.int16),
-            pltpu.VMEM(scales.shape, f32),
+            pltpu.VMEM((slots, rows, LANES), f32),
             pltpu.VMEM((rows, cells), f32),
             pltpu.VMEM((rows, cells), bf16),
             pltpu.VMEM((2 * slots, rows, cells), bf16),
-            dmas, dmas, dmas, dma,
+            dmas, dmas, dma,
         ],
         compiler_params=pltpu.CompilerParams(vmem_limit_bytes=60 * 2**20),
         name="merge_rows",
-    )(kept, codes, scales, info)
+    )(kept, codes, info)
 
 
 def per_device(orbitals, pair_first, pair_second, pair_count):
-    kept, codes, scales, info = exchange(orbitals, pair_first, pair_second, pair_count)
-    return merge(kept, codes, scales, info, orbitals.shape)
+    kept, codes, info = exchange(orbitals, pair_first, pair_second, pair_count)
+    return merge(kept, codes, info, orbitals.shape)
 
 
 def solution(mesh):

time: 48.5 us -> 46.7 us (0.963)
  Pallas kernels: 47.7 us -> 45.9 us
    pallas_call x1, Pallas kernels: 41.9 us -> 40.5 us  [exchange(): pl.pallas_call(functools.partial(pair_kernel, blocks, slots), out_shape=[...]
where the time goes in v6:
time: 46.7 us; the launch traced here: 46.6 us
  Pallas kernels  45.9 us (98%)
  between operations  0.66 us (1%)
    pallas_call x1, Pallas kernels, exchange(): pl.pallas_call(functools.partial(pair_kernel, blocks, slots), out_shape=[...  40.5 us
    pallas_call x1, Pallas kernels, merge(): pl.pallas_call(functools.partial(merge_kernel, slots // 2, shape[0]), out...  5.39 us

profile of v6, /device:TPU:1, one launch (start us, length us, event | category | flops | bytes accessed | tf_op | source)
XLA Modules:
  0.0 46.6 jit_solution(5383591372811139086)
XLA Ops:
  0.7 40.5 %pair_exchange.1 = (f32[4,32,4096]{2,1,0:T(8,128)}, s16[4,32,4224]{2,1,0:T(8,128)(2,1)}, s32[1,10]{1,0:T(1,128)}) custom-call(bf16[32,32,4096]{2,1,0:T(8,128)(2,1)} %orbitals.1, s32[1,4]{1,0:T(1,128)} %first_in.1, s32[1,4]{1,0:T(1,128)} %second_in.1, s32[1]{0:T(128)S(6)} %copy.10.count_in, bf16[768,256]{1,0:T(8,128)(2,1)} %constant.10.clone.lane_fwd, ...), custom_call_target="tpu_custom_call" | custom-call | tf_op jit(solution)/shard_map/pair_exchange/pallas_call | solution.py:452
  41.2 5.4 %merge_rows.1 = bf16[32,32,4096]{2,1,0:T(8,128)(2,1)} custom-call(f32[4,32,4096]{2,1,0:T(8,128)} %get-tuple-element.8.kept_in, s16[4,32,4224]{2,1,0:T(8,128)(2,1)} %get-tuple-element.9.codes_in, s32[1,10]{1,0:T(1,128)} %get-tuple-element.10.info), custom_call_target="tpu_custom_call" | custom-call | tf_op jit(solution)/shard_map/merge_rows/pallas_call | solution.py:632

commit v7 on v6

--- a/solution.py
+++ b/solution.py
@@ -133,7 +133,7 @@
     orb, sending, arriving, sharing, whole, kept, codes,
     spectra, planes, result,
     lane_fwd_v, lane_inv_v, row_fwd_v, row_inv_v, filters_v, twiddles_v, first_s, second_s, count_s,
-    next_second, next_count, relay_second, relay_count, final_here, relay_send, relay_recv, load_sem,
+    next_second, next_count, relay_second, relay_count, final_here, left_here, relay_send, relay_recv, load_sem,
     table_sem, index_send, index_recv, orbital_send, orbital_recv,
     share_send, share_recv, code_send, code_recv, kept_sem, kept_send, kept_recv,
 ):
@@ -143,14 +143,14 @@
     to_partner = {"grid": 1 - core}
 
     final, relay = blocks - 1, max(2, blocks // 4) - 1
-    is_first, is_final = me == 0, me == final
+    is_first, is_final, before_final = me == 0, me == final, me == final - 1
     sends_index, is_relay = core == 1, (me == relay) & (core == 1)
     barrier = pltpu.get_barrier_semaphore()
     for place in range(2):
         pl.semaphore_signal(barrier, inc=1, device_id={"blk": left, "grid": place})
     pl.semaphore_signal(barrier, inc=1, device_id=to_partner)
 
-    @pl.when(jnp.logical_not(is_final))
+    @pl.when(jnp.logical_not(is_final | before_final))
     def _():
         for place in range(2):
             pl.semaphore_signal(barrier, inc=1, device_id={"blk": right, "grid": place})
@@ -242,14 +242,20 @@
         for m in range(half):
             sending[m] = orb[next_second[0, m]]
 
-    normal = 5 + is_final.astype(jnp.int32)
+    normal = 5 - is_final.astype(jnp.int32)
     pl.semaphore_wait(barrier, jnp.where(is_first, 3 + core, normal))
+
+    @pl.when(before_final)
+    def _():
+        for place in range(2):
+            pl.semaphore_signal(left_here, inc=1, device_id={"blk": right, "grid": place})
 
     @pl.when(is_final)
     def _():
         for place in range(2):
             pl.semaphore_signal(final_here, inc=1, device_id={"blk": right, "grid": place})
         pl.semaphore_signal(final_here, inc=1, device_id={"blk": relay, "grid": 1})
+        pl.semaphore_wait(left_here, 2)
 
     @pl.when(is_first)
     def _():
@@ -382,7 +388,8 @@
 
         live = jnp.where(m < jnp.where(core == 0, count_s[0], next_count[0]), 1.0, 0.0).astype(f32)
 
-        def inverse_group(place, carry):
+        def inverse_group(turn, carry):
+            place = 2 * (1 - lax.rem(turn, 2)) + lax.div(turn, 2)
             rows = pl.ds(pl.multiple_of(16 * place, 16), 16)
             high, low = split(planes[:, rows, :].reshape(ROWS * 16, 2 * LANES))
             out = dot(jnp.concatenate([high, low, high], 1), lane_inv_v[...])
@@ -482,7 +489,7 @@
             pltpu.SMEM(pair_count.shape, jnp.int32),
             pltpu.SMEM(pair_second.shape, jnp.int32),
             pltpu.SMEM(pair_count.shape, jnp.int32),
-            pltpu.SemaphoreType.REGULAR, dmas(2, 2), dmas(2), dmas(LOADS),
+            pltpu.SemaphoreType.REGULAR, pltpu.SemaphoreType.REGULAR, dmas(2, 2), dmas(2), dmas(LOADS),
             dmas(9), dmas(2, 2), dmas(2), dmas(slots, 2), dmas(half, 4),
             dmas(half), dmas(half), dmas(half, 4), dmas(slots, 2),
             dmas(half), dmas(half), dmas(half),

time: 46.7 us -> 44 us (0.942)
  the two profiles are of different devices: /device:TPU:1 before, /device:TPU:0 now
where the time goes in v7:
time: 44 us; the launch traced here: 43.8 us
  Pallas kernels  43.1 us (98%)
  between operations  0.66 us (2%)
    pallas_call x1, Pallas kernels, exchange(): pl.pallas_call(functools.partial(pair_kernel, blocks, slots), out_shape=[...  39.1 us
    pallas_call x1, Pallas kernels, merge(): pl.pallas_call(functools.partial(merge_kernel, slots // 2, shape[0]), out...  4.01 us

profile of v7, /device:TPU:0, one launch (start us, length us, event | category | flops | bytes accessed | tf_op | source)
XLA Modules:
  0.0 43.8 jit_solution(9803891516791086144)
XLA Ops:
  0.7 39.1 %pair_exchange.1 = (f32[4,32,4096]{2,1,0:T(8,128)}, s16[4,32,4224]{2,1,0:T(8,128)(2,1)}, s32[1,10]{1,0:T(1,128)}) custom-call(bf16[32,32,4096]{2,1,0:T(8,128)(2,1)} %orbitals.1, s32[1,4]{1,0:T(1,128)} %first_in.1, s32[1,4]{1,0:T(1,128)} %second_in.1, s32[1]{0:T(128)S(6)} %copy.10.count_in, bf16[768,256]{1,0:T(8,128)(2,1)} %constant.10.clone.lane_fwd, ...), custom_call_target="tpu_custom_call" | custom-call | tf_op jit(solution)/shard_map/pair_exchange/pallas_call | solution.py:459
  39.8 4.0 %merge_rows.1 = bf16[32,32,4096]{2,1,0:T(8,128)(2,1)} custom-call(f32[4,32,4096]{2,1,0:T(8,128)} %get-tuple-element.8.kept_in, s16[4,32,4224]{2,1,0:T(8,128)(2,1)} %get-tuple-element.9.codes_in, s32[1,10]{1,0:T(1,128)} %get-tuple-element.10.info), custom_call_target="tpu_custom_call" | custom-call | tf_op jit(solution)/shard_map/merge_rows/pallas_call | solution.py:639

commit v8 on v7

--- a/solution.py
+++ b/solution.py
@@ -503,7 +503,7 @@
 
 def merge_kernel(
     half, block, kept_in, codes_in, info,
-    out, kept, codes, scales, total, zero, staged, kept_sem, code_sem, out_sem,
+    out, kept, codes, scales, total, zero, staged, single, goes_to, kept_sem, code_sem, out_sem,
 ):
     slots = 2 * half
     first = [info[0, slot] for slot in range(slots)]
@@ -558,74 +558,99 @@
         return codes[m, :, lanes].astype(f32) * scales[m, :, 0:1]
 
     def add_up(place, kind_half, lead, live, rows, extra):
-        several = jnp.bool_(False)
+        def begin(lanes):
+            total[:, lanes] = term(kind_half(lead), lead, lanes)
+
+        over_pieces(begin)
         for later in range(lead + 1, slots):
-            several |= live(later) & (rows[later] == rows[lead])
+
+            @pl.when(live(later) & (rows[later] == rows[lead]))
+            def _():
+                def more(lanes):
+                    total[:, lanes] += term(kind_half(later), later, lanes)
+
+                over_pieces(more)
+
         for flag, other in extra:
-            several |= flag
-
-        @pl.when(jnp.logical_not(several))
-        def _():
-            def only(lanes):
-                staged[place, :, lanes] = term(kind_half(lead), lead, lanes).astype(bf16)
-
-            over_pieces(only)
-
-        @pl.when(several)
-        def _():
-            def begin(lanes):
-                total[:, lanes] = term(kind_half(lead), lead, lanes)
-
-            over_pieces(begin)
-            for later in range(lead + 1, slots):
-
-                @pl.when(live(later) & (rows[later] == rows[lead]))
-                def _():
-                    def more(lanes):
-                        total[:, lanes] += term(kind_half(later), later, lanes)
-
-                    over_pieces(more)
-
-            for flag, other in extra:
-
-                @pl.when(flag)
-                def _():
-                    def more(lanes):
-                        total[:, lanes] += staged[other, :, lanes].astype(f32)
-
-                    over_pieces(more)
-
-            def end(lanes):
-                staged[place, :, lanes] = total[:, lanes].astype(bf16)
-
-            over_pieces(end)
-
-    leads = []
+
+            @pl.when(flag)
+            def _():
+                def more(lanes):
+                    total[:, lanes] += staged[other, :, lanes].astype(f32)
+
+                over_pieces(more)
+
+        def end(lanes):
+            staged[place, :, lanes] = total[:, lanes].astype(bf16)
+
+        over_pieces(end)
+
+    def alone(n, carry):
+        m = lax.rem(n, slots)
+        is_kept = (n < slots) == (m >= half)
+
+        @pl.when((single[n] == 1) & is_kept)
+        def _():
+            for piece in range(2):
+                lanes = pl.ds(CELLS // 2 * piece, CELLS // 2)
+                staged[n, :, lanes] = kept[m, :, lanes].astype(bf16)
+
+        @pl.when((single[n] == 1) & jnp.logical_not(is_kept))
+        def _():
+            for piece in range(2):
+                lanes = pl.ds(CELLS // 2 * piece, CELLS // 2)
+                staged[n, :, lanes] = (codes[m, :, lanes].astype(f32) * scales[m, :, 0:1]).astype(bf16)
+
+        @pl.when(goes_to[n] >= 0)
+        def _():
+            pltpu.make_async_copy(staged.at[n], out.at[goes_to[n]], out_sem).start()
+
+        return carry
+
+    def plan(n, lead, several, has_row, row):
+        single[n] = (lead & jnp.logical_not(several)).astype(jnp.int32)
+        goes_to[n] = jnp.where(lead & jnp.logical_not(several) & has_row, row, -1)
+
+    leads, sums = [], []
     for slot in range(slots):
-        lead = back_live(slot)
+        lead, several, owned = back_live(slot), jnp.bool_(False), jnp.bool_(False)
         for earlier in range(slot):
             lead &= second[earlier] != second[slot]
+        for later in range(slot + 1, slots):
+            several |= back_live(later) & (second[later] == second[slot])
+        for other in range(slots):
+            owned |= own_live(other) & (first[other] == second[slot])
         leads.append(lead)
-
-        @pl.when(lead)
+        sums.append((lead & several, owned))
+        plan(slot, lead, several, jnp.logical_not(owned), second[slot])
+    lax.fori_loop(0, slots, alone, 0)
+    for slot, (several, owned) in enumerate(sums):
+
+        @pl.when(several)
         def _():
             add_up(slot, lambda s: s >= half, slot, back_live, second, [])
-            owned = jnp.bool_(False)
-            for other in range(slots):
-                owned |= own_live(other) & (first[other] == second[slot])
 
             @pl.when(jnp.logical_not(owned))
             def _():
                 pltpu.make_async_copy(staged.at[slot], out.at[second[slot]], out_sem).start()
 
+    sums = []
     for slot in range(slots):
-        lead = own_live(slot)
+        lead, several = own_live(slot), jnp.bool_(False)
         for earlier in range(slot):
             lead &= first[earlier] != first[slot]
-
-        @pl.when(lead)
-        def _():
-            extra = [(leads[other] & (second[other] == first[slot]), other) for other in range(slots)]
+        for later in range(slot + 1, slots):
+            several |= own_live(later) & (first[later] == first[slot])
+        extra = [(leads[other] & (second[other] == first[slot]), other) for other in range(slots)]
+        for flag, other in extra:
+            several |= flag
+        sums.append((lead & several, extra))
+        plan(slots + slot, lead, several, jnp.bool_(True), first[slot])
+    lax.fori_loop(slots, 2 * slots, alone, 0)
+    for slot, (several, extra) in enumerate(sums):
+
+        @pl.when(several)
+        def _():
             add_up(slots + slot, lambda s: s < half, slot, own_live, first, extra)
             pltpu.make_async_copy(staged.at[slots + slot], out.at[first[slot]], out_sem).start()
 
@@ -648,6 +673,8 @@
             pltpu.VMEM((rows, cells), f32),
             pltpu.VMEM((rows, cells), bf16),
             pltpu.VMEM((2 * slots, rows, cells), bf16),
+            pltpu.SMEM((2 * slots,), jnp.int32),
+            pltpu.SMEM((2 * slots,), jnp.int32),
             dmas, dmas, dma,
         ],
         compiler_params=pltpu.CompilerParams(vmem_limit_bytes=60 * 2**20),

time: 44 us -> 44.5 us (1.011)
  Pallas kernels: 43.1 us -> 43.6 us
    pallas_call x1, Pallas kernels: 4.01 us -> 4.49 us  [merge(): pl.pallas_call(functools.partial(merge_kernel, slots // 2, shape[0]), out...]
where the time goes in v8:
time: 44.5 us; the launch traced here: 44.2 us
  Pallas kernels  43.6 us (98%)
  between operations  0.66 us (1%)
    pallas_call x1, Pallas kernels, exchange(): pl.pallas_call(functools.partial(pair_kernel, blocks, slots), out_shape=[...  39.1 us
    pallas_call x1, Pallas kernels, merge(): pl.pallas_call(functools.partial(merge_kernel, slots // 2, shape[0]), out...  4.49 us

profile of v8, /device:TPU:0, one launch (start us, length us, event | category | flops | bytes accessed | tf_op | source)
XLA Modules:
  0.0 44.2 jit_solution(16860862064666642840)
XLA Ops:
  0.7 39.1 %pair_exchange.1 = (f32[4,32,4096]{2,1,0:T(8,128)}, s16[4,32,4224]{2,1,0:T(8,128)(2,1)}, s32[1,10]{1,0:T(1,128)}) custom-call(bf16[32,32,4096]{2,1,0:T(8,128)(2,1)} %orbitals.1, s32[1,4]{1,0:T(1,128)} %first_in.1, s32[1,4]{1,0:T(1,128)} %second_in.1, s32[1]{0:T(128)S(6)} %copy.10.count_in, bf16[768,256]{1,0:T(8,128)(2,1)} %constant.10.clone.lane_fwd, ...), custom_call_target="tpu_custom_call" | custom-call | tf_op jit(solution)/shard_map/pair_exchange/pallas_call | solution.py:459
  39.8 4.5 %merge_rows.1 = bf16[32,32,4096]{2,1,0:T(8,128)(2,1)} custom-call(f32[4,32,4096]{2,1,0:T(8,128)} %get-tuple-element.8.kept_in, s16[4,32,4224]{2,1,0:T(8,128)(2,1)} %get-tuple-element.9.codes_in, s32[1,10]{1,0:T(1,128)} %get-tuple-element.10.info), custom_call_target="tpu_custom_call" | custom-call | tf_op jit(solution)/shard_map/merge_rows/pallas_call | solution.py:664

commit v9 on v8

--- a/solution.py
+++ b/solution.py
@@ -522,7 +522,9 @@
         kept_live, code_live = (own_live(m), back_live(m)) if m < half else (back_live(m), own_live(m))
         loads.append((kept_live, pltpu.make_async_copy(kept_in.at[m], kept.at[m], kept_sem.at[m])))
         loads.append((code_live, pltpu.make_async_copy(codes_in.at[m], codes.at[m], code_sem.at[m])))
-    for needed, load in loads:
+    back_loads = loads[1:slots:2] + loads[slots::2]
+    own_loads = loads[0:slots:2] + loads[slots + 1 :: 2]
+    for needed, load in back_loads + own_loads:
         pl.when(needed)(load.start)
     zero[...] = jnp.zeros_like(zero)
 
@@ -536,14 +538,16 @@
         def _():
             pltpu.make_async_copy(zero, out.at[row], out_sem).start()
 
-    for needed, load in loads:
-        pl.when(needed)(load.wait)
-    for m in range(slots):
-        @pl.when(back_live(m) if m < half else own_live(m))
-        def _():
-            side = codes[m, :, CELLS:].astype(f32)
-            scale = scale_of(side[:, :1], side[:, LANES // 2 : LANES // 2 + 1])
-            scales[m] = jnp.broadcast_to(scale, scales.shape[1:])
+    def arrive(some_loads, messages, live):
+        for needed, load in some_loads:
+            pl.when(needed)(load.wait)
+        for m in messages:
+
+            @pl.when(live(m))
+            def _():
+                side = codes[m, :, CELLS:].astype(f32)
+                scale = scale_of(side[:, :1], side[:, LANES // 2 : LANES // 2 + 1])
+                scales[m] = jnp.broadcast_to(scale, scales.shape[1:])
 
     def over_pieces(body):
         def piece(index, carry):
@@ -623,6 +627,7 @@
         leads.append(lead)
         sums.append((lead & several, owned))
         plan(slot, lead, several, jnp.logical_not(owned), second[slot])
+    arrive(back_loads, range(half), back_live)
     lax.fori_loop(0, slots, alone, 0)
     for slot, (several, owned) in enumerate(sums):
 
@@ -646,6 +651,7 @@
             several |= flag
         sums.append((lead & several, extra))
         plan(slots + slot, lead, several, jnp.bool_(True), first[slot])
+    arrive(own_loads, range(half, slots), own_live)
     lax.fori_loop(slots, 2 * slots, alone, 0)
     for slot, (several, extra) in enumerate(sums):
 

time: 44.5 us -> 44.3 us (level)
  no operation moved by 1% of the time
where the time goes in v9:
time: 44.3 us; the launch traced here: 44 us
  Pallas kernels  43.3 us (98%)
  between operations  0.66 us (1%)
    pallas_call x1, Pallas kernels, exchange(): pl.pallas_call(functools.partial(pair_kernel, blocks, slots), out_shape=[...  39.1 us
    pallas_call x1, Pallas kernels, merge(): pl.pallas_call(functools.partial(merge_kernel, slots // 2, shape[0]), out...  4.25 us

profile of v9, /device:TPU:0, one launch (start us, length us, event | category | flops | bytes accessed | tf_op | source)
XLA Modules:
  0.0 44.0 jit_solution(5497870635528296639)
XLA Ops:
  0.7 39.1 %pair_exchange.1 = (f32[4,32,4096]{2,1,0:T(8,128)}, s16[4,32,4224]{2,1,0:T(8,128)(2,1)}, s32[1,10]{1,0:T(1,128)}) custom-call(bf16[32,32,4096]{2,1,0:T(8,128)(2,1)} %orbitals.1, s32[1,4]{1,0:T(1,128)} %first_in.1, s32[1,4]{1,0:T(1,128)} %second_in.1, s32[1]{0:T(128)S(6)} %copy.10.count_in, bf16[768,256]{1,0:T(8,128)(2,1)} %constant.10.clone.lane_fwd, ...), custom_call_target="tpu_custom_call" | custom-call | tf_op jit(solution)/shard_map/pair_exchange/pallas_call | solution.py:459
  39.8 4.2 %merge_rows.1 = bf16[32,32,4096]{2,1,0:T(8,128)(2,1)} custom-call(f32[4,32,4096]{2,1,0:T(8,128)} %get-tuple-element.8.kept_in, s16[4,32,4224]{2,1,0:T(8,128)(2,1)} %get-tuple-element.9.codes_in, s32[1,10]{1,0:T(1,128)} %get-tuple-element.10.info), custom_call_target="tpu_custom_call" | custom-call | tf_op jit(solution)/shard_map/merge_rows/pallas_call | solution.py:670
